TPU v7x, 256 devices: a whole 4x4x8 slice. The times are simulated.
256 devices in a mesh: wave: 64 (over x, z, core), lev: 4 (over y).
Axes of the slice: x: 4, y: 4, z: 8, core: 2. Of those that a mesh axis runs over, the one named last changes fastest.
Arguments:
- fourier: bfloat16 [2, 2, 72, 1280, 640], P(None, None, 'lev', 'wave'), may hold values from -6 to 6
- lat_order: int32 [1280], replicated, may hold values from 0 to 1279, each once
- wave_order: int32 [640], replicated, may hold values from 0 to 639, as said below
- pattern: int32 [64, 64], replicated, may hold values from 0 to 1, as said below
- legendre: bfloat16 [640, 640, 640], P('wave'), may hold values from -0.25 to 0.25
- lat_weight: float32 [640], replicated, may hold values from 0.2 to 1.8
- hydrostatic_thermal_link: float32 [72, 72], replicated, may hold values from -0.75 to 0.75
- evec: float32 [72, 72], replicated, may hold values from -0.75 to 0.75
- einv: float32 [72, 72], replicated, may hold values from -0.75 to 0.75
- spread_to_heat_link: float32 [72, 72], replicated, may hold values from -0.75 to 0.75
- modes: float32 [72], replicated, may hold values from 0.5 to 50
Outputs:
- new_fourier: bfloat16 [2, 2, 72, 1280, 640], P(None, None, 'lev', 'wave')
Inputs may be any that keep to these rules, and one draw needn't show every extreme that they name: `wave_order`: each wavenumber appears once; positions 2i and 2i+1 hold a wavenumber p and 639-p. pattern[i, j] is 1 where j >= i and 0 where j < i - 1.
All inputs are finite; a program needn't handle non-finite values.
Results may differ from a plain program's by a relative error of at most 0.0061.
Values may be sent and summed in bfloat16 or wider, within the bound.
No kernel may reach another device: no remote copies, remote signals or barrier semaphores. Data moves between devices by JAX's collectives and lax.ppermute only.
A program may use at most 128 MiB of HBM per device.

v0:
```python
import jax
import jax.numpy as jnp
from jax import lax
from jax.sharding import PartitionSpec as P

M = 640


def level_apply(matrix, values):
    return jnp.einsum("og,kcgn->kcon", matrix, values, precision=lax.Precision.HIGHEST)


def solve_levels(
    spectra, degree_rows, hydrostatic_thermal_link, evec, einv, spread_to_heat_link, modes
):
    velocity_spread = spectra[:, 0].astype(jnp.float32)
    thermal_state = spectra[:, 1].astype(jnp.float32)
    factor = (degree_rows * (degree_rows + 1)).astype(jnp.float32) / float(M * (M + 1))
    factor = factor[None, None, None, :]
    source_drive = velocity_spread + factor * level_apply(hydrostatic_thermal_link, thermal_state)
    modal_part = level_apply(einv, source_drive) / (1.0 + factor * modes[None, None, :, None])
    next_spread = level_apply(evec, modal_part)
    next_thermal = thermal_state - level_apply(spread_to_heat_link, next_spread)
    return jnp.stack([next_spread, next_thermal], axis=1).astype(jnp.bfloat16)


def local(
    fourier,
    lat_order,
    wave_order,
    pattern,
    legendre,
    lat_weight,
    hydrostatic_thermal_link,
    evec,
    einv,
    spread_to_heat_link,
    modes,
):
    m_local = legendre.shape[0]
    lat_half = legendre.shape[2]
    lat_count = 2 * lat_half
    block_count = pattern.shape[0]
    block_width = M // block_count
    my_waves = lax.dynamic_slice_in_dim(wave_order, lax.axis_index("wave") * m_local, m_local)
    degrees = jnp.arange(M, dtype=jnp.int32)
    parity_even = (degrees[None, :] - my_waves[:, None]) % 2 == 0
    owner_rows = (
        my_waves[:, None] // block_width == jnp.arange(block_count, dtype=jnp.int32)[None, :]
    ).astype(jnp.float32)
    live_rows = jnp.dot(owner_rows, pattern.astype(jnp.float32), precision=lax.Precision.HIGHEST)
    live_mask = jnp.repeat(live_rows, block_width, axis=1)
    half_ids = jnp.arange(lat_half, dtype=jnp.int32)
    north_pick = (lat_order[:, None] == half_ids[None, :]).astype(jnp.bfloat16)
    south_pick = (lat_order[:, None] == (lat_count - 1 - half_ids)[None, :]).astype(jnp.bfloat16)
    north_place = (half_ids[:, None] == lat_order[None, :]).astype(jnp.bfloat16)
    south_place = ((lat_count - 1 - half_ids)[:, None] == lat_order[None, :]).astype(jnp.bfloat16)
    wave_onehot = (degrees[:, None] == wave_order[None, :]).astype(jnp.bfloat16)
    weight = lat_weight[None, None, None, None, :]
    parity_wide = parity_even[:, None, None, None, :]
    live_wide = live_mask[:, None, None, None, :]
    field_count, part_count, lev_local, lat_local = (
        fourier.shape[0],
        fourier.shape[1],
        fourier.shape[2],
        fourier.shape[3],
    )
    flat_in = fourier.reshape(-1, M)
    picked = lax.dot_general(
        wave_onehot, flat_in, (((0,), (1,)), ((), ())), preferred_element_type=jnp.float32
    )
    picked = picked.astype(jnp.bfloat16).reshape(M, field_count, part_count, lev_local, lat_local)
    arrived = lax.all_to_all(picked, "wave", split_axis=0, concat_axis=4, tiled=True)
    north_vals = jnp.dot(arrived, north_pick, preferred_element_type=jnp.float32)
    south_vals = jnp.dot(arrived, south_pick, preferred_element_type=jnp.float32)
    sym_part = ((north_vals + south_vals) * weight).astype(jnp.bfloat16)
    anti_part = ((north_vals - south_vals) * weight).astype(jnp.bfloat16)
    lead = arrived.shape[:4]
    sym_flat = sym_part.reshape(lead[0], -1, lat_half)
    anti_flat = anti_part.reshape(lead[0], -1, lat_half)
    sym_terms = jnp.einsum(
        "kxh,knh->kxn", sym_flat, legendre, preferred_element_type=jnp.float32
    ).reshape(lead + (M,))
    anti_terms = jnp.einsum(
        "kxh,knh->kxn", anti_flat, legendre, preferred_element_type=jnp.float32
    ).reshape(lead + (M,))
    chosen = jnp.where(parity_wide, sym_terms, anti_terms)
    harmonic_amplitudes = chosen * live_wide
    harmonic_amplitudes = harmonic_amplitudes.astype(jnp.bfloat16)
    lev_count = lax.axis_size("lev")
    quarter = M // lev_count
    shifted = lax.all_to_all(harmonic_amplitudes, "lev", split_axis=4, concat_axis=3, tiled=True)
    degree_rows = lax.axis_index("lev") * quarter + jnp.arange(quarter, dtype=jnp.int32)
    solved = solve_levels(
        shifted, degree_rows, hydrostatic_thermal_link, evec, einv, spread_to_heat_link, modes
    )
    returned_spec = lax.all_to_all(solved, "lev", split_axis=3, concat_axis=4, tiled=True)
    masked = returned_spec * live_wide.astype(jnp.bfloat16)
    signed_vals = masked * jnp.where(parity_wide, 1.0, -1.0).astype(jnp.bfloat16)
    masked_flat = masked.reshape(m_local, -1, M)
    signed_flat = signed_vals.reshape(m_local, -1, M)
    north_new = jnp.einsum(
        "kxn,knh->kxh", masked_flat, legendre, preferred_element_type=jnp.float32
    ).astype(jnp.bfloat16)
    south_new = jnp.einsum(
        "kxn,knh->kxh", signed_flat, legendre, preferred_element_type=jnp.float32
    ).astype(jnp.bfloat16)
    banded = jnp.dot(north_new, north_place, preferred_element_type=jnp.float32) + jnp.dot(
        south_new, south_place, preferred_element_type=jnp.float32
    )
    banded = banded.astype(jnp.bfloat16).reshape(
        m_local, field_count, part_count, lev_local, lat_count
    )
    returned = lax.all_to_all(banded, "wave", split_axis=4, concat_axis=0, tiled=True)
    flat_back = returned.reshape(M, -1)
    restored = lax.dot_general(
        flat_back, wave_onehot, (((0,), (1,)), ((), ())), preferred_element_type=jnp.float32
    )
    return restored.astype(jnp.bfloat16).reshape(fourier.shape)


def solution(mesh):
    placed = (
        P(None, None, "lev", "wave", None),
        P(),
        P(),
        P(),
        P("wave", None, None),
        P(),
        P(),
        P(),
        P(),
        P(),
        P(),
    )
    return jax.shard_map(
        local,
        mesh=mesh,
        in_specs=placed,
        out_specs=P(None, None, "lev", "wave", None),
        check_vma=False,
    )
```

profile of v0, /device:TPU:1, one launch (start us, length us, event | category | flops | bytes accessed | tf_op | source)
XLA Modules:
  0.0 557.2 jit_solution(13897919907273699825)
XLA Ops:
  0.0 1.8 copy.46
  1.8 0.0 copy-start.6
  1.8 1.9 reshape.141
  3.8 4.6 convolution_convert_fusion.1
  8.3 2.4 reshape.142
  10.7 18.6 %copy.47 = bf16[640,2,2,18,20]{4,2,3,1,0:T(2,128)(2,1)} copy(bf16[640,2,2,18,20]{0,4,3,2,1:T(8,128)(2,1)S(1)} %reshape.142) | data formatting | bytes 3686400 | tf_op jit(solution)/shard_map/reshape | solution.py:72
  29.4 32.1 %reshape.160 = bf16[64,2,7200]{2,1,0:T(2,128)(2,1)} reshape(bf16[640,2,18,2,20]{4,3,2,1,0:T(2,128)(2,1)} %bitcast.112) | data formatting | bytes 3686400
  61.5 13.5 %all-to-all-start = ((bf16[64,2,7200]{2,1,0:T(2,128)(2,1)}), bf16[64,2,7200]{2,1,0:T(2,128)(2,1)S(1)}, u32[]{:S(2)}, u32[]{:S(2)}) async-start(bf16[64,2,7200]{2,1,0:T(2,128)(2,1)} %reshape.160), calls=%async_computation | async-start | bytes 3735552 | tf_op jit(solution)/shard_map/all_to_all | solution.py:73
  75.0 0.1 and_select_fusion
  75.1 0.2 fusion.58
  75.3 0.2 broadcast_in_dim.14
  75.4 0.2 mul.87
  75.7 0.1 fusion.50
  75.8 45.3 %all-to-all-done = bf16[64,2,7200]{2,1,0:T(2,128)(2,1)S(1)} async-done(((bf16[64,2,7200]{2,1,0:T(2,128)(2,1)}), bf16[64,2,7200]{2,1,0:T(2,128)(2,1)S(1)}, u32[]{:S(2)}, u32[]{:S(2)}) %all-to-all-start) | async-done | bytes 1843232 | tf_op jit(solution)/shard_map/all_to_all | solution.py:73
  121.1 14.4 %reshape.161 = bf16[640,2,18,2,20]{4,3,2,1,0:T(2,128)(2,1)} reshape(bf16[64,2,7200]{2,1,0:T(2,128)(2,1)S(1)} %all-to-all-done) | data formatting | bytes 3686400
  135.4 11.1 %copy.73 = bf16[10,2,2,18,64,20]{5,4,3,2,1,0:T(8,128)(2,1)} copy(bf16[10,2,2,18,64,20]{5,2,3,1,0,4:T(2,128)(2,1)} %bitcast.113) | data formatting | bytes 3686400 | tf_op jit(solution)/shard_map/all_to_all | solution.py:73
  146.5 22.0 %reshape.159 = bf16[10,2,2,18,1280]{4,3,2,1,0:T(8,128)(2,1)S(1)} reshape(bf16[10,2,2,18,64,20]{5,4,3,2,1,0:T(8,128)(2,1)} %copy.73) | data formatting | bytes 3686400 | tf_op jit(solution)/shard_map/all_to_all | solution.py:73
  168.6 0.0 copy-start.9
  168.6 2.3 fusion.7
  170.9 3.8 multiply_convert_fusion.1
  174.7 1.4 reshape.145
  176.1 7.6 %fusion.65 = f32[10,72,640]{2,1,0:T(8,128)} fusion(bf16[10,72,640]{2,1,0:T(8,128)(2,1)S(1)} %reshape.145, bf16[10,640,640]{2,1,0:T(8,128)(2,1)} %param.15), kind=kOutput, calls=%fused_computation.79 | convolution fusion | flops 589824000 | bytes 10956800 | tf_op jit(solution)/shard_map/kxh,knh->kxn/dot_general | solution.py:84
  183.7 1.6 reshape.146
  185.3 1.4 reshape.143
  186.7 7.6 %fusion.64 = f32[10,72,640]{2,1,0:T(8,128)} fusion(bf16[10,72,640]{2,1,0:T(8,128)(2,1)S(1)} %reshape.143, bf16[10,640,640]{2,1,0:T(8,128)(2,1)} %param.15), kind=kOutput, calls=%fused_computation.78 | convolution fusion | flops 589824000 | bytes 10956800 | tf_op jit(solution)/shard_map/kxh,knh->kxn/dot_general | solution.py:81
  194.3 2.8 reshape.144
  197.0 3.3 multiply_convert_fusion
  200.3 13.4 %copy.51 = bf16[10,2,2,18,640]{3,2,1,0,4:T(2,128)(2,1)} copy(bf16[10,2,2,18,640]{4,3,2,1,0:T(8,128)(2,1)} %multiply_convert_fusion) | data formatting | bytes 1843200 | tf_op jit(solution)/shard_map/convert_element_type | solution.py:89
  213.7 14.7 %reshape.162 = bf16[4,2,57600]{2,1,0:T(2,128)(2,1)} reshape(bf16[640,10,2,2,18]{4,3,2,1,0:T(2,128)(2,1)} %bitcast.114) | data formatting | bytes 1843200
  228.4 12.6 %all-to-all-start.1 = ((bf16[4,2,57600]{2,1,0:T(2,128)(2,1)}), bf16[4,2,57600]{2,1,0:T(2,128)(2,1)S(1)}, u32[]{:S(2)}, u32[]{:S(2)}) async-start(bf16[4,2,57600]{2,1,0:T(2,128)(2,1)} %reshape.162), calls=%async_computation.1 | async-start | bytes 1843200 | tf_op jit(solution)/shard_map/all_to_all | solution.py:92
  241.0 0.1 multiply_add_fusion
  241.1 13.0 %all-to-all-done.1 = bf16[4,2,57600]{2,1,0:T(2,128)(2,1)S(1)} async-done(((bf16[4,2,57600]{2,1,0:T(2,128)(2,1)}), bf16[4,2,57600]{2,1,0:T(2,128)(2,1)S(1)}, u32[]{:S(2)}, u32[]{:S(2)}) %all-to-all-start.1) | async-done | bytes 921632 | tf_op jit(solution)/shard_map/all_to_all | solution.py:92
  254.1 18.2 %reshape.163 = bf16[640,10,2,2,18]{4,3,2,1,0:T(2,128)(2,1)} reshape(bf16[4,2,57600]{2,1,0:T(2,128)(2,1)S(1)} %all-to-all-done.1) | data formatting | bytes 1843200
  272.3 14.0 %copy.69 = bf16[10,2,2,18,4,160]{5,4,2,3,1,0:T(4,128)(2,1)S(1)} copy(bf16[10,2,2,18,4,160]{3,2,1,0,5,4:T(2,128)(2,1)} %bitcast.115) | data formatting | bytes 1843200 | tf_op jit(solution)/shard_map/all_to_all | solution.py:92
  286.3 1.2 copy.53
  287.6 0.0 copy-start.2
  287.6 1.0 fusion.63
  288.6 0.7 fusion.42
  289.4 0.0 copy-start.7
  289.4 1.6 fusion.18
  291.0 1.5 fusion.22
  292.5 0.0 copy-start.3
  292.5 0.1 fusion.39
  292.6 0.7 copy-done.3
  293.3 1.6 fusion.27
  294.9 0.3 pad_maximum_fusion
  295.2 2.2 copy.56
  297.4 3.8 all-to-all-start.2
  301.2 0.1 select_convert_fusion
  301.3 18.0 %all-to-all-done.2 = bf16[10,2,2,72,160]{4,2,0,1,3:T(2,128)(2,1)S(1)} async-done(((bf16[10,2,2,72,160]{4,2,0,1,3:T(2,128)(2,1)}), bf16[10,2,2,72,160]{4,2,0,1,3:T(2,128)(2,1)S(1)}, u32[]{:S(2)}, u32[]{:S(2)}) %all-to-all-start.2) | async-done | bytes 921632 | tf_op jit(solution)/shard_map/all_to_all | solution.py:97
  319.3 0.8 copy.58
  320.1 0.9 all_to_all.61
  321.0 8.2 %fusion.5 = f32[10,72,1280]{2,1,0:T(8,128)} fusion(s32[1280]{0:T(1024)S(1)} %copy-done.4, bf16[10,640,640]{2,1,0:T(8,128)(2,1)} %param.15, bf16[10,72,640]{2,1,0:T(8,128)(2,1)S(1)} %all_to_all.61, bf16[10,640]{1,0:T(8,128)(2,1)S(1)} %convert_element_type.73), kind=kOutput, calls=%fused_computation.7 | convolution fusion | flops 1771212800 | bytes 12817920 | tf_op jit(solution)/shard_map/dot_general | solution.py:108
  329.2 8.8 %fusion = bf16[10,72,1280]{2,1,0:T(8,128)(2,1)} fusion(f32[10,72,1280]{2,1,0:T(8,128)} %fusion.5, s32[1280]{0:T(1024)S(1)} %copy-done.4, s32[640]{0:T(1024)S(1)} %iota_subtract_fusion, bf16[10,640,640]{2,1,0:T(8,128)(2,1)} %param.15, bf16[10,72,640]{2,1,0:T(8,128)(2,1)S(1)} %all_to_all.61, bf16[10,640]{1,0:T(8,128)(2,1)S(1)} %select_convert_fusion, ...), kind=kOutput, calls=%fused_computation.1 | convolution fusion | flops 1773516800 | bytes 14676480 | tf_op jit(solution)/shard_map/dot_general | solution.py:108
  338.0 2.5 reshape.147
  340.5 20.4 %copy.59 = bf16[10,2,2,18,1280]{3,2,1,0,4:T(2,128)(2,1)} copy(bf16[10,2,2,18,1280]{4,3,2,1,0:T(8,128)(2,1)S(1)} %reshape.147) | data formatting | bytes 3686400 | tf_op jit(solution)/shard_map/reshape | solution.py:111
  360.9 31.0 %reshape.164 = bf16[64,2,7200]{2,1,0:T(2,128)(2,1)S(1)} reshape(bf16[1280,10,2,2,18]{4,3,2,1,0:T(2,128)(2,1)} %bitcast.111) | data formatting | bytes 3686400
  391.9 55.2 %all_to_all.69 = bf16[64,2,7200]{2,1,0:T(2,128)(2,1)} all-to-all(bf16[64,2,7200]{2,1,0:T(2,128)(2,1)S(1)} %reshape.164), channel_id=1, replica_groups=mesh['wave'=64,'lev'=4] {'wave'}, dimensions={0} | all-to-all | bytes 3686400 | tf_op jit(solution)/shard_map/all_to_all | solution.py:114
  447.1 43.1 %reshape.165 = bf16[1280,10,2,2,18]{4,3,2,1,0:T(2,128)(2,1)} reshape(bf16[64,2,7200]{2,1,0:T(2,128)(2,1)} %all_to_all.69) | data formatting | bytes 3686400
  490.3 40.3 %copy.72 = bf16[10,2,2,18,64,20]{5,3,2,1,0,4:T(8,128)(2,1)} copy(bf16[10,2,2,18,64,20]{3,2,1,0,5,4:T(2,128)(2,1)} %bitcast.110) | data formatting | bytes 3686400 | tf_op jit(solution)/shard_map/all_to_all | solution.py:114
  530.6 17.9 %reshape.148 = bf16[640,1440]{1,0:T(8,128)(2,1)S(1)} reshape(bf16[64,10,2,2,18,20]{5,4,3,2,1,0:T(8,128)(2,1)} %bitcast.109) | data formatting | bytes 3686400 | tf_op jit(solution)/shard_map/reshape | solution.py:115
  548.5 3.2 convolution_convert_fusion
  551.6 2.4 reshape.149
  554.1 2.7 copy.62
  (17 shorter events, 0.0 us)
Async XLA Ops:
  0.0 288.6 %copy-start = (f32[72,72]{1,0:T(8,128)S(1)}, f32[72,72]{1,0:T(8,128)}, u32[]{:S(2)}) copy-start(f32[72,72]{1,0:T(8,128)} %param.17) | copy-start | bytes 62212
  1.8 1.9 copy-start.6
  61.5 13.6 %copy-start.8 = (s32[64,64]{1,0:T(8,128)S(1)}, s32[64,64]{1,0:T(8,128)}, u32[]{:S(2)}) copy-start(s32[64,64]{1,0:T(8,128)} %param.14) | copy-start | bytes 49156
  61.5 59.6 %all-to-all-start = ((bf16[64,2,7200]{2,1,0:T(2,128)(2,1)}), bf16[64,2,7200]{2,1,0:T(2,128)(2,1)S(1)}, u32[]{:S(2)}, u32[]{:S(2)}) async-start(bf16[64,2,7200]{2,1,0:T(2,128)(2,1)} %reshape.160), calls=%async_computation | async-start | bytes 3735552 | tf_op jit(solution)/shard_map/all_to_all | solution.py:73
  146.5 22.1 %copy-start.4 = (s32[1280]{0:T(1024)S(1)}, s32[1280]{0:T(1024)}, u32[]{:S(2)}) copy-start(s32[1280]{0:T(1024)} %param.12) | copy-start | bytes 15364
  168.6 2.3 copy-start.9
  213.7 27.3 %copy-start.5 = (f32[72]{0:T(128)S(1)}, f32[72]{0:T(128)}, u32[]{:S(2)}) copy-start(f32[72]{0:T(128)} %param.21) | copy-start | bytes 868
  228.4 25.7 %all-to-all-start.1 = ((bf16[4,2,57600]{2,1,0:T(2,128)(2,1)}), bf16[4,2,57600]{2,1,0:T(2,128)(2,1)S(1)}, u32[]{:S(2)}, u32[]{:S(2)}) async-start(bf16[4,2,57600]{2,1,0:T(2,128)(2,1)} %reshape.162), calls=%async_computation.1 | async-start | bytes 1843200 | tf_op jit(solution)/shard_map/all_to_all | solution.py:92
  287.6 1.8 copy-start.2
  289.4 1.6 copy-start.7
  292.5 0.8 copy-start.3
  297.4 21.8 %all-to-all-start.2 = ((bf16[10,2,2,72,160]{4,2,0,1,3:T(2,128)(2,1)}), bf16[10,2,2,72,160]{4,2,0,1,3:T(2,128)(2,1)S(1)}, u32[]{:S(2)}, u32[]{:S(2)}) async-start(bf16[10,2,2,72,160]{4,2,0,1,3:T(2,128)(2,1)} %copy.56), calls=%async_computation.2 | async-start | bytes 2949120 | tf_op jit(solution)/shard_map/all_to_all | solution.py:97
  551.6 5.1 copy-start.1
where the time goes:
time: 567 us; the launch traced here: 557 us
  local copies, waits for them, and re-layouts  340 us (60%)
  waiting for transfers between devices  76.3 us (13%)
  blocking collectives  55.2 us (10%)
  matrix products  51.5 us (9%)
  starting transfers between devices  29.9 us (5%)
    unnamed x27, local copies, waits for them, and re-layouts  156 us
    all_to_all x1, blocking collectives, local(): lax.all_to_all(banded, 'wave', split_axis=4, concat_axis=0, tiled=True)  55.2 us
    all_to_all x1, waiting for transfers between devices, local(): lax.all_to_all(picked, 'wave', split_axis=0, concat_axis=4, tiled=True)  45.3 us
    all_to_all x1, local copies, waits for them, and re-layouts, local(): lax.all_to_all(banded, 'wave', split_axis=4, concat_axis=0, tiled=True)  40.3 us
    all_to_all x2, local copies, waits for them, and re-layouts, local(): lax.all_to_all(picked, 'wave', split_axis=0, concat_axis=4, tiled=True)  33.1 us
    reshape x2, local copies, waits for them, and re-layouts, local(): banded.astype(jnp.bfloat16)  23 us
    reshape x2, local copies, waits for them, and re-layouts, local(): picked.astype(jnp.bfloat16)  21 us
    all_to_all x1, waiting for transfers between devices, local(): lax.all_to_all(solved, 'lev', split_axis=3, concat_axis=4, tiled=True)  18 us
  transfers between devices with their start and end apart: 3, of which 3 were waited for; matrix products, arithmetic and copies ran while one was open for 0% of the time, Pallas kernels for 0%

commit v1 on v0

v1 whole, which is shorter than its diff:
```python
import jax
import jax.numpy as jnp
from jax import lax
from jax.experimental import pallas as pl
from jax.experimental.pallas import tpu as pltpu
from jax.sharding import PartitionSpec as P

RQ, R5 = 4, 5
ROWS = 8
LANES = 512
LEV = 4
LOCAL = 18
X = LEV * LOCAL
FL = 2 * LOCAL
UNIT = 40
XP = LEV * UNIT
SHARE = 5
GROUP = R5 * UNIT
WIDE = 2 * LANES
CUTS = 2
NT = (((1,), (1,)), ((), ()))
TN = (((0,), (0,)), ((), ()))
NN = (((1,), (0,)), ((), ()))
F32 = jnp.float32
BF16 = jnp.bfloat16


def dot(a, b, dims):
    return lax.dot_general(a, b, dims, preferred_element_type=F32)


def params(mebibytes):
    return pltpu.CompilerParams(vmem_limit_bytes=mebibytes * 1024 * 1024)


def put_rows(scr, start, size, stride, values):
    width = scr.shape[2]
    for t in range(scr.shape[0]):
        scr[t, pl.ds(start, size, stride=stride), :] = values[:, t * width : (t + 1) * width]


def get_rows(scr, start, size, stride):
    tiles = [scr[t, pl.ds(start, size, stride=stride), :] for t in range(scr.shape[0])]
    return jnp.concatenate(tiles, axis=1)


def put_block(scr, block):
    width = scr.shape[2]
    for t in range(scr.shape[0]):
        part = block[:, :, t * width : (t + 1) * width].astype(F32)
        scr[t] = part.reshape(scr.shape[1:])


def send_block(scr, out_buf, out_hbm, out_sem):
    width = scr.shape[2]
    peers, rows = out_buf.shape[0], out_buf.shape[1]
    step = peers // CUTS
    stores = []
    for cut in range(CUTS):
        part = pl.ds(cut * step, step)
        for t in range(scr.shape[0]):
            piece = scr[t, pl.ds(cut * step * rows, step * rows), :].reshape(step, rows, width)
            out_buf[part, :, pl.ds(t * width, width)] = piece.astype(BF16)
        stores.append(pltpu.make_async_copy(out_buf.at[part], out_hbm.at[part], out_sem.at[cut]))
        stores[-1].start()
    for store in stores:
        store.wait()


def tiles_of(size):
    return (size // 128, 128) if size % 128 == 0 else (1, size)


def h_block(lat_half):
    return 128 if lat_half % 128 == 0 else lat_half


def wave_matrix(wave_ref, peers):
    count = wave_ref.shape[0]
    m_local = count // peers
    row = lax.broadcasted_iota(jnp.int32, (count, 1), 0)
    ids = lax.broadcasted_iota(jnp.int32, (count, count), 1)
    slot = lax.rem(row, peers) * m_local + lax.div(row, peers)
    waves = wave_ref[...].reshape(1, count).astype(F32)
    held = jnp.sum(jnp.where(ids == slot, waves, 0.0), axis=1, keepdims=True)
    return jnp.where(held == ids.astype(F32), 1.0, 0.0).astype(BF16)


def fill_lat_matrix(rows_ref, ot_scr):
    lat_count = ot_scr.shape[0]
    half = lat_count // 2
    hb = h_block(half)
    at = rows_ref.shape[0] - 3
    lats = jnp.concatenate([rows_ref[at : at + 1, :], rows_ref[at + 1 : at + 2, :]], axis=1)
    lats = lats.astype(jnp.int32)
    for block in range(half // hb):
        ids = lax.broadcasted_iota(jnp.int32, (hb, lat_count), 0) + block * hb
        north = jnp.where(lats == ids, 1.0, 0.0).astype(BF16)
        south = jnp.where(lats == lat_count - 1 - ids, 1.0, 0.0).astype(BF16)
        ot_scr[2 * block * hb : (2 * block + 1) * hb, :] = north
        ot_scr[(2 * block + 1) * hb : (2 * block + 2) * hb, :] = south


def pieces_of(peer):
    pieces = []
    for combo in range(SHARE * peer, SHARE * (peer + 1)):
        kk, c = combo // 2, combo % 2
        if pieces and pieces[-1][0] == kk:
            pieces[-1] = (kk, 0, 2)
        else:
            pieces.append((kk, c, c + 1))
    return pieces


def select_kernel(wave_ref, x_hbm, out_hbm, x_buf, x_scr, z_scr, scr, out_buf, in_sem, out_sem):
    waves = z_scr.shape[1]
    peers = out_buf.shape[0] // LEV
    loads = []
    for rq in range(RQ):
        part = pl.ds(rq * R5, R5)
        loads.append(pltpu.make_async_copy(x_hbm.at[:, part], x_buf.at[:, part], in_sem.at[rq]))
        loads[-1].start()
    onehot = wave_matrix(wave_ref, peers)
    for rq in range(RQ):
        loads[rq].wait()
        for r5 in range(R5):
            piece = x_buf[:, rq * R5 + r5].astype(F32).reshape(2 * FL, waves)
            put_rows(x_scr, 0, 2 * FL, 1, piece)
            for c in range(2):
                part = get_rows(x_scr, c, FL, 2)
                part = jnp.concatenate([part, jnp.zeros((UNIT - FL, waves), F32)], axis=0)
                at = c * GROUP + r5 * UNIT
                z_scr[at : at + UNIT, :] = part.astype(BF16)
        got = dot(onehot, z_scr[...], NT)
        for peer in range(LEV):
            parts = [
                got[kk * peers : (kk + 1) * peers, low * GROUP : high * GROUP]
                for kk, low, high in pieces_of(peer)
            ]
            parts.append(jnp.zeros((peers, WIDE - SHARE * GROUP), F32))
            row = jnp.concatenate(parts, axis=1)
            for side in range(2):
                start = peer * ROWS + rq * 2 + side
                put_rows(scr, start, peers, LEV * ROWS, row[:, side * LANES : (side + 1) * LANES])
    send_block(scr, out_buf, out_hbm, out_sem)


def split(values):
    high = values.astype(BF16)
    return high, (values - high.astype(F32)).astype(BF16)


def spectral_kernel(
    place_ref, r_ref, rows_ref, vert_ref, leg_hbm, out_ref,
    ot_scr, scr, lat_scr, sa_scr, band_scr, leg_buf, leg_sem,
):
    peers = r_ref.shape[0] // LEV
    half = ot_scr.shape[0] // 2
    hb = h_block(half)
    span = 2 * peers
    waves = rows_ref.shape[1]
    me = place_ref[place_ref.shape[0] - 1]
    odd_me = lax.rem(me, 2)
    base = lax.div(me * SHARE, 2)
    loads = []
    for i in range(leg_buf.shape[0]):
        loads.append(pltpu.make_async_copy(leg_hbm.at[base + i], leg_buf.at[i], leg_sem.at[i]))
        loads[-1].start()
    fill_lat_matrix(rows_ref, ot_scr)
    put_block(scr, r_ref[...])
    for p in range(LEV):
        for pair in range(RQ // 2):
            part = jnp.concatenate(
                [
                    jnp.concatenate(
                        [get_rows(scr, p * ROWS + 2 * rq + side, peers, LEV * ROWS) for side in range(2)],
                        axis=1,
                    )
                    for rq in (2 * pair, 2 * pair + 1)
                ],
                axis=0,
            )
            turned = part.T
            for j in range(SHARE):
                for r5 in range(R5):
                    at = (j * R5 + r5) * UNIT
                    lane = (r5 * 2 + pair) * span
                    lat_scr[j, p * UNIT : (p + 1) * UNIT, lane : lane + span] = turned[at : at + UNIT].astype(BF16)
    lhs = lat_scr[...].reshape(SHARE * XP, 2 * half)
    for block in range(half // hb):
        both = dot(lhs, ot_scr[2 * block * hb : (2 * block + 2) * hb, :], NT)
        north, south = both[:, :hb], both[:, hb:]
        weight = rows_ref[rows_ref.shape[0] - 1 :, block * hb : (block + 1) * hb]
        sym = ((north + south) * weight).astype(BF16)
        anti = ((north - south) * weight).astype(BF16)
        sa_scr[:, :XP, block * hb : (block + 1) * hb] = sym.reshape(SHARE, XP, hb)
        sa_scr[:, XP:, block * hb : (block + 1) * hb] = anti.reshape(SHARE, XP, hb)

    first_high, first_low = split(vert_ref[: 2 * X, :])
    second_high, second_low = split(vert_ref[2 * X :, :X])
    keep = vert_ref[2 * X :, X : X + 1]
    modes = vert_ref[2 * X : 3 * X, X + 1 : X + 2]
    degree = lax.broadcasted_iota(jnp.int32, (1, waves), 1)
    factor = (degree * (degree + 1)).astype(F32) / float(waves * (waves + 1))
    scale = 1.0 + factor * modes
    for load in loads:
        load.wait()
    for j in range(SHARE):
        slot = lax.div(j + odd_me, 2)
        live = rows_ref[pl.ds(base + slot, 1), :]
        even = lax.rem(degree + place_ref[base + slot], 2) == 0
        leg = leg_buf[slot]
        terms = dot(sa_scr[j], leg, NT)
        state_low = (jnp.where(even, terms[:XP], terms[XP:]) * live).astype(BF16)
        state = state_low.astype(F32)
        mixed = dot(first_high, state_low, NN) + dot(first_low, state_low, NN)
        modal = (mixed[:X] + factor * mixed[X:]) / scale
        modal_high, modal_low = split(modal)
        new = (
            dot(second_high, modal_high, NN)
            + dot(second_high, modal_low, NN)
            + dot(second_low, modal_high, NN)
        )
        new = (new + keep * state).astype(BF16).astype(F32) * live
        signed = jnp.where(even, new, -new)
        grid = dot(jnp.concatenate([new, signed], axis=0).astype(BF16), leg, NN).astype(BF16)
        for block in range(half // hb):
            piece = grid[:, block * hb : (block + 1) * hb]
            lat_scr[j, :, 2 * block * hb : (2 * block + 1) * hb] = piece[:XP]
            lat_scr[j, :, (2 * block + 1) * hb : (2 * block + 2) * hb] = piece[XP:]

    lhs = lat_scr[...].reshape(SHARE * XP, 2 * half)
    for r5 in range(R5):
        band = dot(lhs, ot_scr[:, 2 * r5 * span : 2 * (r5 + 1) * span], NN)
        for j in range(SHARE):
            for p in range(LEV):
                at = (j * R5 + r5) * UNIT
                row = j * XP + p * UNIT
                band_scr[p, at : at + UNIT, :] = band[row : row + UNIT]
    for p in range(LEV):
        for pair in range(RQ // 2):
            turned = band_scr[p, :, pair * span : (pair + 1) * span].T
            for i in range(2):
                for side in range(2):
                    start = p * ROWS + (2 * pair + i) * 2 + side
                    piece = turned[i * peers : (i + 1) * peers, side * LANES : (side + 1) * LANES]
                    put_rows(scr, start, peers, LEV * ROWS, piece)
    width = scr.shape[2]
    for t in range(scr.shape[0]):
        part = scr[t].reshape(out_ref.shape[:2] + (width,))
        out_ref[:, :, t * width : (t + 1) * width] = part.astype(BF16)


def restore_kernel(wave_ref, r_ref, out_hbm, scr, y_scr, out_buf, out_sem):
    peers = r_ref.shape[0] // LEV
    waves = wave_ref.shape[0]
    onehot = wave_matrix(wave_ref, peers)
    put_block(scr, r_ref[...])
    stores = []
    for rq in range(RQ):
        held = {}
        for peer in range(LEV):
            row = jnp.concatenate(
                [get_rows(scr, peer * ROWS + rq * 2 + side, peers, LEV * ROWS) for side in range(2)],
                axis=1,
            )
            at = 0
            for kk, low, high in pieces_of(peer):
                size = (high - low) * GROUP
                held.setdefault(kk, []).append(row[:, at : at + size])
                at += size
        parts = [jnp.concatenate(held[kk], axis=1) for kk in sorted(held)]
        part = jnp.concatenate(parts, axis=0).astype(BF16)
        got = dot(part, onehot, TN)
        for r5 in range(R5):
            for c in range(2):
                at = c * GROUP + r5 * UNIT
                put_rows(y_scr, c, FL, 2, got[at : at + FL])
            piece = get_rows(y_scr, 0, 2 * FL, 1).astype(BF16)
            out_buf[:, rq * R5 + r5] = piece.reshape(FL, 2, waves)
        part = pl.ds(rq * R5, R5)
        stores.append(pltpu.make_async_copy(out_buf.at[:, part], out_hbm.at[:, part], out_sem.at[rq]))
        stores[-1].start()
    for store in stores:
        store.wait()


def local(
    fourier,
    lat_order,
    wave_order,
    pattern,
    legendre,
    lat_weight,
    hydrostatic_thermal_link,
    evec,
    einv,
    spread_to_heat_link,
    modes,
):
    m_local, waves, lat_half = legendre.shape
    lat_count = 2 * lat_half
    count = waves // m_local
    block_count = pattern.shape[0]
    block_width = waves // block_count
    high = lax.Precision.HIGHEST

    lat_rows = lat_order.reshape(count, RQ, R5).transpose(2, 1, 0).reshape(2, lat_half).astype(F32)
    my_waves = lax.dynamic_slice_in_dim(wave_order, lax.axis_index("wave") * m_local, m_local)
    owner_rows = (
        my_waves[:, None] // block_width == jnp.arange(block_count, dtype=jnp.int32)[None, :]
    ).astype(F32)
    live_rows = jnp.dot(owner_rows, pattern.astype(F32), precision=high)
    live = jnp.repeat(live_rows, block_width, axis=1)
    rows_in = jnp.concatenate([live, lat_rows, lat_weight[None, :]], axis=0)
    places = jnp.concatenate([my_waves, lax.axis_index("lev")[None]]).astype(jnp.int32)

    einv_link = jnp.dot(einv, hydrostatic_thermal_link, precision=high)
    heat_evec = jnp.dot(spread_to_heat_link, evec, precision=high)
    gap = ((0, 0), (0, UNIT - FL), (0, 0))
    none = jnp.zeros((X, LEV, LOCAL), F32)
    tail = jnp.zeros((X, LEV, UNIT - FL), F32)
    first = jnp.concatenate(
        [
            jnp.concatenate([einv.reshape(X, LEV, LOCAL), none, tail], axis=2),
            jnp.concatenate([none, einv_link.reshape(X, LEV, LOCAL), tail], axis=2),
        ],
        axis=0,
    ).reshape(2 * X, XP)
    second = jnp.concatenate(
        [evec.reshape(LEV, LOCAL, X), -heat_evec.reshape(LEV, LOCAL, X)], axis=1
    )
    second = jnp.pad(second, gap).reshape(XP, X)
    place = jnp.arange(XP, dtype=jnp.int32) % UNIT
    keep = ((place >= LOCAL) & (place < FL)).astype(F32)[:, None]
    column = jnp.arange(XP, dtype=jnp.int32)[None, :]
    second = jnp.pad(second, ((0, 0), (0, XP - X))) + keep * (column == X).astype(F32)
    second = second + jnp.pad(modes, (0, XP - X))[:, None] * (column == X + 1).astype(F32)
    vert = jnp.concatenate([first, second], axis=0)

    vmem = pl.BlockSpec(memory_space=pltpu.VMEM)
    smem = pl.BlockSpec(memory_space=pltpu.SMEM)
    hbm = pl.BlockSpec(memory_space=pltpu.HBM)
    peers = count * LEV
    rowed = (FL, RQ * R5, 2, waves)
    block = jax.ShapeDtypeStruct((peers, ROWS, LANES), BF16)
    block_scratch = pltpu.VMEM((LANES // 128, peers * ROWS, 128), F32)
    lane_tiles, lane_width = tiles_of(waves)
    row_scratch = pltpu.VMEM((lane_tiles, 2 * FL, lane_width), F32)

    sent = pl.pallas_call(
        select_kernel,
        in_specs=[vmem, hbm],
        out_specs=hbm,
        out_shape=block,
        scratch_shapes=[
            pltpu.VMEM(rowed, BF16),
            row_scratch,
            pltpu.VMEM((2 * GROUP, waves), BF16),
            block_scratch,
            pltpu.VMEM(block.shape, BF16),
            pltpu.SemaphoreType.DMA((RQ,)),
            pltpu.SemaphoreType.DMA((CUTS,)),
        ],
        compiler_params=params(60),
        name="select_waves",
    )(wave_order, fourier.transpose(0, 2, 3, 1, 4).reshape(rowed))
    arrived = lax.all_to_all(sent, ("wave", "lev"), split_axis=0, concat_axis=0, tiled=True)
    solved = pl.pallas_call(
        spectral_kernel,
        in_specs=[smem] + [vmem] * 3 + [hbm],
        out_specs=vmem,
        out_shape=block,
        scratch_shapes=[
            pltpu.VMEM((lat_count, lat_count), BF16),
            block_scratch,
            pltpu.VMEM((SHARE, XP, lat_count), BF16),
            pltpu.VMEM((SHARE, 2 * XP, lat_half), BF16),
            pltpu.VMEM((LEV, WIDE, RQ * count), F32),
            pltpu.VMEM((3,) + legendre.shape[1:], BF16),
            pltpu.SemaphoreType.DMA((3,)),
        ],
        compiler_params=params(54),
        name="spectral_round",
    )(places, arrived, rows_in, vert, legendre)
    returned = lax.all_to_all(solved, ("wave", "lev"), split_axis=0, concat_axis=0, tiled=True)
    restored = pl.pallas_call(
        restore_kernel,
        in_specs=[vmem] * 2,
        out_specs=hbm,
        out_shape=jax.ShapeDtypeStruct(rowed, BF16),
        scratch_shapes=[
            block_scratch,
            row_scratch,
            pltpu.VMEM(rowed, BF16),
            pltpu.SemaphoreType.DMA((RQ,)),
        ],
        compiler_params=params(48),
        name="restore_waves",
    )(wave_order, returned)
    restored = restored.reshape(2, LOCAL, RQ * R5, 2, waves)
    return restored.transpose(0, 3, 1, 2, 4)


def solution(mesh):
    placed = (
        P(None, None, "lev", "wave", None),
        P(),
        P(),
        P(),
        P("wave", None, None),
        P(),
        P(),
        P(),
        P(),
        P(),
        P(),
    )
    return jax.shard_map(
        local,
        mesh=mesh,
        in_specs=placed,
        out_specs=P(None, None, "lev", "wave", None),
        check_vma=False,
    )
```

time: 567 us -> 174 us (0.31); the launches traced: 557 us -> 174 us
  local copies, waits for them, and re-layouts: 340 us -> 2.41 us
  matrix products: 51.5 us -> 0.65 us
  Pallas kernels: 0 us -> 40.1 us
  waiting for transfers between devices: 76.3 us -> 50.4 us
  starting transfers between devices: 29.9 us -> 15.8 us
  blocking collectives: 55.2 us -> 61.5 us
    unnamed x27 -> x21, local copies, waits for them, and re-layouts: 156 us -> 1.46 us
    all_to_all x7 -> x0, local copies, waits for them, and re-layouts: 90.4 us -> none  [the longest x1 40.3 us: local(): lax.all_to_all(banded, 'wave', split_axis=4, concat_axis=0, tiled=True)]
    reshape x12 -> x5, local copies, waits for them, and re-layouts: 76.1 us -> 0.33 us  [the longest x1 0.21 us: local(): live = jnp.repeat(live_rows, block_width, axis=1)]
    dot_general x13 -> x3, matrix products: 51.5 us -> 0.65 us  [the longest x1 0.26 us: local(): einv_link = jnp.dot(einv, hydrostatic_thermal_link, precision=high)]
    pallas_call x0 -> x3, Pallas kernels: none -> 40.1 us  [the longest x1 23.6 us: local(): pl.pallas_call(spectral_kernel, in_specs=[smem] + [vmem] * 3 + [hbm], out...]
    all_to_all x3 -> x1, waiting for transfers between devices: 76.3 us -> 50.4 us  [local(): lax.all_to_all(sent, ('wave', 'lev'), split_axis=0, concat_axis=0, tiled=...]
    all_to_all x3 -> x1, starting transfers between devices: 29.9 us -> 15.8 us  [local(): lax.all_to_all(sent, ('wave', 'lev'), split_axis=0, concat_axis=0, tiled=...]
    convert_element_type x1 -> x3, local copies, waits for them, and re-layouts: 13.4 us -> 0.44 us  [local(): lat_order.reshape(count, RQ, R5).transpose(2, 1, 0).reshape(2, lat_half)]
  transfers between devices with their start and end apart: 3 -> 1, of which waited for: 3 -> 1; matrix products, arithmetic and copies ran while one was open for 0% -> 2% of each run, Pallas kernels for 0% -> 0%
where the time goes in v1:
time: 174 us
  blocking collectives  61.5 us (35%)
  waiting for transfers between devices  50.4 us (29%)
  Pallas kernels  40.1 us (23%)
  starting transfers between devices  15.8 us (9%)
  local copies, waits for them, and re-layouts  2.41 us (1%)
  other arithmetic  2.39 us (1%)
    all_to_all x1, blocking collectives, local(): lax.all_to_all(solved, ('wave', 'lev'), split_axis=0, concat_axis=0, tile...  61.5 us
    all_to_all x1, waiting for transfers between devices, local(): lax.all_to_all(sent, ('wave', 'lev'), split_axis=0, concat_axis=0, tiled=...  50.4 us
    pallas_call x1, Pallas kernels, local(): pl.pallas_call(spectral_kernel, in_specs=[smem] + [vmem] * 3 + [hbm], out...  23.6 us
    all_to_all x1, starting transfers between devices, local(): lax.all_to_all(sent, ('wave', 'lev'), split_axis=0, concat_axis=0, tiled=...  15.8 us
    pallas_call x1, Pallas kernels, local(): pl.pallas_call(select_kernel, in_specs=[vmem, hbm], out_specs=hbm, out_sh...  10.3 us
    pallas_call x1, Pallas kernels, local(): pl.pallas_call(restore_kernel, in_specs=[vmem] * 2, out_specs=hbm, out_sh...  6.19 us
  transfers between devices with their start and end apart: 1, of which 1 were waited for; matrix products, arithmetic and copies ran while one was open for 2% of the time, Pallas kernels for 0%

profile of v1, /device:TPU:1, one launch (start us, length us, event | category | flops | bytes accessed | tf_op | source)
XLA Modules:
  0.0 173.7 jit_solution(3953528613613608106)
XLA Ops:
  0.0 0.0 copy-start
  0.0 10.3 %select_waves.1 = bf16[256,8,512]{2,1,0:T(8,128)(2,1)} custom-call(s32[640]{0:T(1024)} %wave_ref.3, bf16[36,20,2,640]{3,2,1,0:T(2,128)(2,1)} %bitcast.18), custom_call_target="tpu_custom_call" | custom-call | tf_op jit(solution)/shard_map/select_waves/pallas_call | solution.py:351
  10.3 0.0 copy-start.7
  10.3 0.0 copy-start.6
  10.4 0.0 copy-start.1
  10.4 0.0 copy-start.9
  10.4 0.0 copy-start.4
  10.4 0.0 copy-start.3
  10.4 0.0 copy-start.5
  10.4 0.0 copy-start.8
  10.4 15.8 %all-to-all-start = ((bf16[256,8,512]{2,1,0:T(8,128)(2,1)}), bf16[256,8,512]{2,1,0:T(8,128)(2,1)S(1)}, u32[]{:S(2)}, u32[]{:S(2)}) async-start(bf16[256,8,512]{2,1,0:T(8,128)(2,1)} %select_waves.1), calls=%async_computation | async-start | bytes 4194304 | tf_op jit(solution)/shard_map/all_to_all | solution.py:368
  26.3 0.0 copy-done.7
  26.3 0.0 copy-done.6
  26.3 0.2 convert_element_type.47
  26.6 0.1 copy.12
  26.7 0.1 convert_element_type.49
  26.8 0.0 copy-done.1
  26.8 0.1 and_select_fusion.1
  26.9 0.0 copy-done.9
  26.9 0.2 fusion
  27.1 0.2 broadcast_in_dim.21
  27.2 0.2 reshape.68
  27.5 0.0 copy-done.4
  27.5 0.0 copy-done
  27.5 0.2 convolution_negate_fusion
  27.7 0.0 copy-done.3
  27.7 0.1 copy.13
  27.8 0.0 copy-done.5
  27.8 0.3 fusion.3
  28.1 0.0 copy-done.8
  28.1 0.1 maximum_maximum_fusion
  28.3 0.1 copy.15
  28.4 0.7 pad_add_fusion.place_ref
  29.1 0.6 pad_maximum_fusion.1.rows_ref
  29.7 0.1 multiply_add_fusion
  29.8 0.7 pad_maximum_fusion.vert_ref
  30.6 50.4 %all-to-all-done.r_ref = bf16[256,8,512]{2,1,0:T(8,128)(2,1)S(1)} async-done(((bf16[256,8,512]{2,1,0:T(8,128)(2,1)}), bf16[256,8,512]{2,1,0:T(8,128)(2,1)S(1)}, u32[]{:S(2)}, u32[]{:S(2)}) %all-to-all-start) | async-done | bytes 2097184 | tf_op jit(solution)/shard_map/all_to_all | solution.py:368
  80.9 0.0 copy-start.2
  80.9 1.3 copy-done.2
  82.3 23.6 %spectral_round.1 = bf16[256,8,512]{2,1,0:T(8,128)(2,1)} custom-call(s32[11]{0:T(128)} %pad_add_fusion.place_ref, bf16[256,8,512]{2,1,0:T(8,128)(2,1)} %copy-done.2, f32[13,640]{1,0:T(8,128)} %pad_maximum_fusion.1.rows_ref, f32[304,160]{1,0:T(8,128)} %pad_maximum_fusion.vert_ref, bf16[10,640,640]{2,1,0:T(8,128)(2,1)} %leg_hbm.1), custom_call_target="tpu_custom_call" | custom-call | tf_op jit(solution)/shard_map/spectral_round/pallas_call | solution.py:369
  105.9 61.5 %all_to_all.10.r_ref = bf16[256,8,512]{2,1,0:T(8,128)(2,1)S(1)} all-to-all(bf16[256,8,512]{2,1,0:T(8,128)(2,1)} %spectral_round.1), channel_id=1, replica_groups=mesh['wave'=64,'lev'=4] {'wave','lev'}, dimensions={0} | all-to-all | bytes 4194304 | tf_op jit(solution)/shard_map/all_to_all | solution.py:386
  167.4 6.2 %restore_waves.1 = bf16[36,20,2,640]{3,2,1,0:T(2,128)(2,1)} custom-call(s32[640]{0:T(1024)S(1)} %copy-done.1, bf16[256,8,512]{2,1,0:T(8,128)(2,1)S(1)} %all_to_all.10.r_ref), custom_call_target="tpu_custom_call" | custom-call | tf_op jit(solution)/shard_map/restore_waves/pallas_call | solution.py:387
  (12 shorter events, 0.1 us)
Async XLA Ops:
  0.0 27.5 %copy-start = (f32[72,72]{1,0:T(8,128)S(1)}, f32[72,72]{1,0:T(8,128)}, u32[]{:S(2)}) copy-start(f32[72,72]{1,0:T(8,128)} %param.20) | copy-start | bytes 62212
  10.3 16.0 %copy-start.7 = (f32[640]{0:T(1024)S(1)}, f32[640]{0:T(1024)}, u32[]{:S(2)}) copy-start(f32[640]{0:T(1024)} %param.16) | copy-start | bytes 7684
  10.3 16.0 %copy-start.6 = (s32[1280]{0:T(1024)S(1)}, s32[1280]{0:T(1024)}, u32[]{:S(2)}) copy-start(s32[1280]{0:T(1024)} %param.12) | copy-start | bytes 15364
  10.4 16.4 %copy-start.1 = (s32[640]{0:T(1024)S(1)}, s32[640]{0:T(1024)}, u32[]{:S(2)}) copy-start(s32[640]{0:T(1024)} %wave_ref.3) | copy-start | bytes 7684
  10.4 16.5 %copy-start.9 = (s32[64,64]{1,0:T(8,128)S(1)}, s32[64,64]{1,0:T(8,128)}, u32[]{:S(2)}) copy-start(s32[64,64]{1,0:T(8,128)} %param.14) | copy-start | bytes 49156
  10.4 17.1 %copy-start.4 = (f32[72,72]{1,0:T(8,128)S(1)}, f32[72,72]{1,0:T(8,128)}, u32[]{:S(2)}) copy-start(f32[72,72]{1,0:T(8,128)} %param.18) | copy-start | bytes 62212
  10.4 17.3 %copy-start.3 = (f32[72,72]{1,0:T(8,128)S(1)}, f32[72,72]{1,0:T(8,128)}, u32[]{:S(2)}) copy-start(f32[72,72]{1,0:T(8,128)} %param.19) | copy-start | bytes 62212
  10.4 17.4 %copy-start.5 = (f32[72,72]{1,0:T(8,128)S(1)}, f32[72,72]{1,0:T(8,128)}, u32[]{:S(2)}) copy-start(f32[72,72]{1,0:T(8,128)} %param.17) | copy-start | bytes 62212
  10.4 17.7 %copy-start.8 = (f32[72]{0:T(128)S(1)}, f32[72]{0:T(128)}, u32[]{:S(2)}) copy-start(f32[72]{0:T(128)} %param.21) | copy-start | bytes 868
  10.4 70.5 %all-to-all-start = ((bf16[256,8,512]{2,1,0:T(8,128)(2,1)}), bf16[256,8,512]{2,1,0:T(8,128)(2,1)S(1)}, u32[]{:S(2)}, u32[]{:S(2)}) async-start(bf16[256,8,512]{2,1,0:T(8,128)(2,1)} %select_waves.1), calls=%async_computation | async-start | bytes 4194304 | tf_op jit(solution)/shard_map/all_to_all | solution.py:368
  80.9 1.3 copy-start.2

commit v2 on v1

v2 whole, which is shorter than its diff:
```python
import jax
import jax.numpy as jnp
from jax import lax
from jax.experimental import pallas as pl
from jax.experimental.pallas import tpu as pltpu
from jax.sharding import PartitionSpec as P

RQ, R5 = 4, 5
ROWS = 8
PITCH = 40
LANES = 512
LEV = 4
LOCAL = 18
X = LEV * LOCAL
FL = 2 * LOCAL
UNIT = 40
XP = LEV * UNIT
PAIR = 2 * FL
XW = LEV * PAIR
SIDE = 384
HALF = 2 * SIDE
WIDE = 2 * LANES
TOTAL = 2 * XW + XP
WHOLE = ((0, 1), (3, 4), (5, 6), (8, 9))
SHARED = (2, 7)
CUTS = 2
NT = (((1,), (1,)), ((), ()))
TN = (((0,), (0,)), ((), ()))
NN = (((1,), (0,)), ((), ()))
F32 = jnp.float32
BF16 = jnp.bfloat16


def dot(a, b, dims):
    return lax.dot_general(a, b, dims, preferred_element_type=F32)


def params(mebibytes):
    return pltpu.CompilerParams(vmem_limit_bytes=mebibytes * 1024 * 1024)


def put_rows(scr, start, size, stride, values):
    width = scr.shape[2]
    for t in range(scr.shape[0]):
        scr[t, pl.ds(start, size, stride=stride), :] = values[:, t * width : (t + 1) * width]


def get_rows(scr, start, size, stride):
    tiles = [scr[t, pl.ds(start, size, stride=stride), :] for t in range(scr.shape[0])]
    return jnp.concatenate(tiles, axis=1)


def put_block(scr, block_ref):
    width = scr.shape[2]
    for w in range(block_ref.shape[0] // LEV):
        for t in range(scr.shape[0]):
            part = block_ref[w * LEV : (w + 1) * LEV, :, t * width : (t + 1) * width].astype(F32)
            scr[t, w * PITCH : w * PITCH + LEV * ROWS, :] = part.reshape(LEV * ROWS, width)


def get_block(scr, out_ref, first, last):
    width = scr.shape[2]
    for w in range(first, last):
        for t in range(scr.shape[0]):
            part = scr[t, w * PITCH : w * PITCH + LEV * ROWS, :].reshape(LEV, ROWS, width)
            out_ref[w * LEV : (w + 1) * LEV, :, t * width : (t + 1) * width] = part.astype(BF16)


def send_block(scr, out_buf, out_hbm, out_sem):
    peers = out_buf.shape[0] // LEV
    step = peers // CUTS
    stores = []
    for cut in range(CUTS):
        get_block(scr, out_buf, cut * step, (cut + 1) * step)
        part = pl.ds(cut * step * LEV, step * LEV)
        stores.append(pltpu.make_async_copy(out_buf.at[part], out_hbm.at[part], out_sem.at[cut]))
        stores[-1].start()
    for store in stores:
        store.wait()


def h_block(lat_half):
    return 128 if lat_half % 128 == 0 else lat_half


def wave_matrix(wave_ref, peers):
    count = wave_ref.shape[0]
    m_local = count // peers
    row = lax.broadcasted_iota(jnp.int32, (count, 1), 0)
    ids = lax.broadcasted_iota(jnp.int32, (count, count), 1)
    slot = lax.rem(row, peers) * m_local + lax.div(row, peers)
    waves = wave_ref[...].reshape(1, count).astype(F32)
    held = jnp.sum(jnp.where(ids == slot, waves, 0.0), axis=1, keepdims=True)
    return jnp.where(held == ids.astype(F32), 1.0, 0.0).astype(BF16)


def fill_lat_matrix(rows_ref, ot_scr):
    lat_count = ot_scr.shape[0]
    half = lat_count // 2
    hb = h_block(half)
    at = rows_ref.shape[0] - 3
    lats = jnp.concatenate([rows_ref[at : at + 1, :], rows_ref[at + 1 : at + 2, :]], axis=1)
    lats = lats.astype(jnp.int32)
    for block in range(half // hb):
        ids = lax.broadcasted_iota(jnp.int32, (hb, lat_count), 0) + block * hb
        north = jnp.where(lats == ids, 1.0, 0.0).astype(BF16)
        south = jnp.where(lats == lat_count - 1 - ids, 1.0, 0.0).astype(BF16)
        ot_scr[2 * block * hb : (2 * block + 1) * hb, :] = north
        ot_scr[(2 * block + 1) * hb : (2 * block + 2) * hb, :] = south


def part_matrix():
    row = lax.broadcasted_iota(jnp.int32, (SIDE, 2 * (WIDE - HALF)), 0)
    lane = lax.broadcasted_iota(jnp.int32, (1, 2 * (WIDE - HALF)), 1)
    c = lax.div(lane, WIDE - HALF)
    inner = lax.rem(lane, WIDE - HALF)
    unit, fl = lax.div(inner, UNIT), lax.rem(inner, UNIT)
    source = jnp.where((unit < R5) & (fl < FL), unit * PAIR + fl * 2 + c, -1)
    return jnp.where(row == source, 1.0, 0.0).astype(BF16)


def select_kernel(wave_ref, x_hbm, out_hbm, x_buf, z_scr, scr, out_buf, in_sem, out_sem):
    waves = z_scr.shape[2]
    peers = out_buf.shape[0] // LEV
    loads = []
    for rq in range(RQ):
        part = pl.ds(rq * R5, R5)
        loads.append(pltpu.make_async_copy(x_hbm.at[:, part], x_buf.at[:, part], in_sem.at[rq]))
        loads[-1].start()
    onehot = wave_matrix(wave_ref, peers)
    apart = part_matrix()
    z_scr[:, R5 * PAIR :, :] = jnp.zeros((RQ, SIDE - R5 * PAIR, waves), BF16)
    for rq in range(RQ):
        loads[rq].wait()
        for r5 in range(R5):
            piece = x_buf[:, rq * R5 + r5].reshape(PAIR, waves)
            z_scr[rq, r5 * PAIR : (r5 + 1) * PAIR, :] = piece
    for rq in range(RQ):
        got = dot(onehot, z_scr[rq], NT)

        def put(peer, tile, values):
            for t in range(values.shape[1] // 128):
                side, lane = (tile + t) // 4, (tile + t) % 4
                start = peer * ROWS + rq * 2 + side
                scr[lane, pl.ds(start, peers, stride=PITCH), :] = values[:, t * 128 : (t + 1) * 128]

        for peer in range(LEV):
            for i, kk in enumerate(WHOLE[peer]):
                put(peer, 3 * i, got[kk * peers : (kk + 1) * peers])
        both = jnp.concatenate([got[kk * peers : (kk + 1) * peers] for kk in SHARED], axis=0)
        both = dot(both.astype(BF16), apart, NN)
        for peer in range(LEV):
            rows = both[(peer // 2) * peers : (peer // 2 + 1) * peers]
            put(peer, 6, rows[:, (peer % 2) * (WIDE - HALF) : (peer % 2 + 1) * (WIDE - HALF)])
    send_block(scr, out_buf, out_hbm, out_sem)


def split(values):
    high = values.astype(BF16)
    return high, (values - high.astype(F32)).astype(BF16)


def slots_of(p):
    for i in range(2):
        yield i * SIDE, PAIR, i * XW + p * PAIR
    yield HALF, UNIT, 2 * XW + p * UNIT


def solve(state_low, factor, first, second, keep, modes):
    first_high, first_low = first
    second_high, second_low = second
    size = modes.shape[0]
    mixed = dot(first_high, state_low, NN) + dot(first_low, state_low, NN)
    modal = (mixed[:size] + factor * mixed[size:]) / (1.0 + factor * modes)
    modal_high, modal_low = split(modal)
    new = (
        dot(second_high, modal_high, NN)
        + dot(second_high, modal_low, NN)
        + dot(second_low, modal_high, NN)
    )
    return (new + keep * state_low.astype(F32)).astype(BF16)


def spectral_kernel(
    place_ref, r_ref, rows_ref, vert_ref, wide_ref, leg_hbm, out_ref,
    ot_scr, scr, lat_scr, sym_scr, anti_scr, band_scr, leg_buf, leg_sem,
):
    peers = r_ref.shape[0] // LEV
    half = ot_scr.shape[0] // 2
    hb = h_block(half)
    span = 2 * peers
    waves = rows_ref.shape[1]
    me = place_ref[place_ref.shape[0] - 1]
    whole = lax.div(5 * me + 1, 2)
    held = (whole, whole + 1, 2 + 5 * lax.div(me, 2))
    loads = []
    for i, kk in enumerate(held):
        loads.append(pltpu.make_async_copy(leg_hbm.at[kk], leg_buf.at[i], leg_sem.at[i]))
        loads[-1].start()
    fill_lat_matrix(rows_ref, ot_scr)
    put_block(scr, r_ref)
    for p in range(LEV):
        for pair in range(RQ // 2):
            part = jnp.concatenate(
                [
                    jnp.concatenate(
                        [get_rows(scr, p * ROWS + 2 * rq + side, peers, PITCH) for side in range(2)],
                        axis=1,
                    )
                    for rq in (2 * pair, 2 * pair + 1)
                ],
                axis=0,
            )
            turned = part.T
            for at, size, row in slots_of(p):
                for r5 in range(R5):
                    lane = (r5 * 2 + pair) * span
                    piece = turned[at + r5 * size : at + (r5 + 1) * size]
                    lat_scr[row : row + size, lane : lane + span] = piece.astype(BF16)
    lhs = lat_scr[...]
    for block in range(half // hb):
        both = dot(lhs, ot_scr[2 * block * hb : (2 * block + 2) * hb, :], NT)
        north, south = both[:, :hb], both[:, hb:]
        weight = rows_ref[rows_ref.shape[0] - 1 :, block * hb : (block + 1) * hb]
        sym_scr[:, block * hb : (block + 1) * hb] = ((north + south) * weight).astype(BF16)
        anti_scr[:, block * hb : (block + 1) * hb] = ((north - south) * weight).astype(BF16)

    wide = (
        split(wide_ref[:XW, :]),
        split(wide_ref[XW:, : 2 * X]),
        wide_ref[XW:, 2 * X : 2 * X + 1],
        wide_ref[XW : XW + 2 * X, 2 * X + 1 : 2 * X + 2],
    )
    narrow = (
        split(vert_ref[: 2 * X, :]),
        split(vert_ref[2 * X :, :X]),
        vert_ref[2 * X :, X : X + 1],
        vert_ref[2 * X : 3 * X, X + 1 : X + 2],
    )
    degree = lax.broadcasted_iota(jnp.int32, (1, waves), 1)
    factor = (degree * (degree + 1)).astype(F32) / float(waves * (waves + 1))
    for i, kk in enumerate(held):
        low, size = i * XW, XW if i < 2 else XP
        live = rows_ref[pl.ds(kk, 1), :]
        even = lax.rem(degree + place_ref[kk], 2) == 0
        loads[i].wait()
        leg = leg_buf[i]
        sym = dot(sym_scr[low : low + size, :], leg, NT)
        anti = dot(anti_scr[low : low + size, :], leg, NT)
        state_low = (jnp.where(even, sym, anti) * live).astype(BF16)
        new = solve(state_low, factor, *(wide if i < 2 else narrow)).astype(F32) * live
        signed = jnp.where(even, new, -new)
        north = dot(new.astype(BF16), leg, NN).astype(BF16)
        south = dot(signed.astype(BF16), leg, NN).astype(BF16)
        for block in range(half // hb):
            lane = 2 * block * hb
            lat_scr[low : low + size, lane : lane + hb] = north[:, block * hb : (block + 1) * hb]
            lat_scr[low : low + size, lane + hb : lane + 2 * hb] = south[:, block * hb : (block + 1) * hb]

    lhs = lat_scr[...]
    for r5 in range(R5):
        band = dot(lhs, ot_scr[:, 2 * r5 * span : 2 * (r5 + 1) * span], NN)
        for p in range(LEV):
            for at, size, row in slots_of(p):
                band_scr[p, at + r5 * size : at + (r5 + 1) * size, :] = band[row : row + size]
    for p in range(LEV):
        for pair in range(RQ // 2):
            turned = band_scr[p, :, pair * span : (pair + 1) * span].T
            for i in range(2):
                for side in range(2):
                    start = p * ROWS + (2 * pair + i) * 2 + side
                    piece = turned[i * peers : (i + 1) * peers, side * LANES : (side + 1) * LANES]
                    put_rows(scr, start, peers, PITCH, piece)
    get_block(scr, out_ref, 0, peers)


def restore_kernel(wave_ref, r_ref, out_hbm, scr, out_buf, out_sem):
    peers = r_ref.shape[0] // LEV
    waves = wave_ref.shape[0]
    onehot = wave_matrix(wave_ref, peers)
    apart = part_matrix()
    put_block(scr, r_ref)
    stores = []
    for rq in range(RQ):

        def get(peer, tile, tiles):
            values = []
            for t in range(tile, tile + tiles):
                start = peer * ROWS + rq * 2 + t // 4
                values.append(scr[t % 4, pl.ds(start, peers, stride=PITCH), :])
            return jnp.concatenate(values, axis=1)

        parts = {}
        for peer in range(LEV):
            for i, kk in enumerate(WHOLE[peer]):
                parts[kk] = get(peer, 3 * i, 3)
        lane = lax.broadcasted_iota(jnp.int32, (peers, WIDE - HALF), 1)
        shared = [
            jnp.concatenate(
                [jnp.where(lane < R5 * UNIT, get(2 * i + c, 6, 2), 0.0) for c in range(2)], axis=1
            )
            for i in range(2)
        ]
        shared = dot(jnp.concatenate(shared, axis=0).astype(BF16), apart, NT)
        for i, kk in enumerate(SHARED):
            parts[kk] = shared[i * peers : (i + 1) * peers]
        part = jnp.concatenate([parts[kk] for kk in sorted(parts)], axis=0).astype(BF16)
        got = dot(part, onehot, TN).astype(BF16)
        for r5 in range(R5):
            piece = got[r5 * PAIR : (r5 + 1) * PAIR].reshape(FL, 2, waves)
            out_buf[:, rq * R5 + r5] = piece
        part = pl.ds(rq * R5, R5)
        stores.append(pltpu.make_async_copy(out_buf.at[:, part], out_hbm.at[:, part], out_sem.at[rq]))
        stores[-1].start()
    for store in stores:
        store.wait()


def local(
    fourier,
    lat_order,
    wave_order,
    pattern,
    legendre,
    lat_weight,
    hydrostatic_thermal_link,
    evec,
    einv,
    spread_to_heat_link,
    modes,
):
    m_local, waves, lat_half = legendre.shape
    lat_count = 2 * lat_half
    count = waves // m_local
    block_count = pattern.shape[0]
    block_width = waves // block_count
    high = lax.Precision.HIGHEST

    lat_rows = lat_order.reshape(count, RQ, R5).transpose(2, 1, 0).reshape(2, lat_half).astype(F32)
    my_waves = lax.dynamic_slice_in_dim(wave_order, lax.axis_index("wave") * m_local, m_local)
    owner_rows = (
        my_waves[:, None] // block_width == jnp.arange(block_count, dtype=jnp.int32)[None, :]
    ).astype(F32)
    live_rows = jnp.dot(owner_rows, pattern.astype(F32), precision=high)
    live = jnp.repeat(live_rows, block_width, axis=1)
    rows_in = jnp.concatenate([live, lat_rows, lat_weight[None, :]], axis=0)
    places = jnp.concatenate([my_waves, lax.axis_index("lev")[None]]).astype(jnp.int32)

    einv_link = jnp.dot(einv, hydrostatic_thermal_link, precision=high)
    heat_evec = jnp.dot(spread_to_heat_link, evec, precision=high)
    gap = ((0, 0), (0, UNIT - FL), (0, 0))
    none = jnp.zeros((X, LEV, LOCAL), F32)
    tail = jnp.zeros((X, LEV, UNIT - FL), F32)
    first = jnp.concatenate(
        [
            jnp.concatenate([einv.reshape(X, LEV, LOCAL), none, tail], axis=2),
            jnp.concatenate([none, einv_link.reshape(X, LEV, LOCAL), tail], axis=2),
        ],
        axis=0,
    ).reshape(2 * X, XP)
    second = jnp.concatenate(
        [evec.reshape(LEV, LOCAL, X), -heat_evec.reshape(LEV, LOCAL, X)], axis=1
    )
    second = jnp.pad(second, gap).reshape(XP, X)
    place = jnp.arange(XP, dtype=jnp.int32) % UNIT
    keep = ((place >= LOCAL) & (place < FL)).astype(F32)[:, None]
    column = jnp.arange(XP, dtype=jnp.int32)[None, :]
    second = jnp.pad(second, ((0, 0), (0, XP - X))) + keep * (column == X).astype(F32)
    second = second + jnp.pad(modes, (0, XP - X))[:, None] * (column == X + 1).astype(F32)
    vert = jnp.concatenate([first, second], axis=0)

    twin = jnp.eye(2, dtype=F32)
    none = jnp.zeros((X, LEV, LOCAL), F32)
    fold = jnp.stack(
        [
            jnp.concatenate([einv.reshape(X, LEV, LOCAL), none], axis=2),
            jnp.concatenate([none, einv_link.reshape(X, LEV, LOCAL)], axis=2),
        ]
    ).reshape(2, X, 1, LEV, FL, 1)
    wide_first = (fold * twin.reshape(1, 1, 2, 1, 1, 2)).reshape(4 * X, XW)
    spread = jnp.concatenate(
        [evec.reshape(LEV, LOCAL, X), -heat_evec.reshape(LEV, LOCAL, X)], axis=1
    ).reshape(X * 2, 1, X, 1)
    wide_second = (spread * twin.reshape(1, 2, 1, 2)).reshape(XW, 2 * X)
    place = (jnp.arange(XW, dtype=jnp.int32) % PAIR) // 2
    keep = (place >= LOCAL).astype(F32)[:, None]
    column = jnp.arange(XW, dtype=jnp.int32)[None, :]
    wide_second = jnp.pad(wide_second, ((0, 0), (0, XW - 2 * X))) + keep * (column == 2 * X).astype(F32)
    modes_twin = jnp.pad(jnp.repeat(modes, 2), (0, XW - 2 * X))[:, None]
    wide_second = wide_second + modes_twin * (column == 2 * X + 1).astype(F32)
    wide_vert = jnp.concatenate([wide_first, wide_second], axis=0)

    vmem = pl.BlockSpec(memory_space=pltpu.VMEM)
    smem = pl.BlockSpec(memory_space=pltpu.SMEM)
    hbm = pl.BlockSpec(memory_space=pltpu.HBM)
    peers = count * LEV
    rowed = (FL, RQ * R5, 2, waves)
    block = jax.ShapeDtypeStruct((peers, ROWS, LANES), BF16)
    block_scratch = pltpu.VMEM((LANES // 128, count * PITCH, 128), F32)

    sent = pl.pallas_call(
        select_kernel,
        in_specs=[vmem, hbm],
        out_specs=hbm,
        out_shape=block,
        scratch_shapes=[
            pltpu.VMEM(rowed, BF16),
            pltpu.VMEM((RQ, SIDE, waves), BF16),
            block_scratch,
            pltpu.VMEM(block.shape, BF16),
            pltpu.SemaphoreType.DMA((RQ,)),
            pltpu.SemaphoreType.DMA((CUTS,)),
        ],
        compiler_params=params(60),
        name="select_waves",
    )(wave_order, fourier.transpose(0, 2, 3, 1, 4).reshape(rowed))
    arrived = lax.all_to_all(sent, ("wave", "lev"), split_axis=0, concat_axis=0, tiled=True)
    solved = pl.pallas_call(
        spectral_kernel,
        in_specs=[smem] + [vmem] * 4 + [hbm],
        out_specs=vmem,
        out_shape=block,
        scratch_shapes=[
            pltpu.VMEM((lat_count, lat_count), BF16),
            block_scratch,
            pltpu.VMEM((TOTAL, lat_count), BF16),
            pltpu.VMEM((TOTAL, lat_half), BF16),
            pltpu.VMEM((TOTAL, lat_half), BF16),
            pltpu.VMEM((LEV, WIDE, RQ * count), F32),
            pltpu.VMEM((3,) + legendre.shape[1:], BF16),
            pltpu.SemaphoreType.DMA((3,)),
        ],
        compiler_params=params(46),
        name="spectral_round",
    )(places, arrived, rows_in, vert, wide_vert, legendre)
    returned = lax.all_to_all(solved, ("wave", "lev"), split_axis=0, concat_axis=0, tiled=True)
    restored = pl.pallas_call(
        restore_kernel,
        in_specs=[vmem] * 2,
        out_specs=hbm,
        out_shape=jax.ShapeDtypeStruct(rowed, BF16),
        scratch_shapes=[
            block_scratch,
            pltpu.VMEM(rowed, BF16),
            pltpu.SemaphoreType.DMA((RQ,)),
        ],
        compiler_params=params(48),
        name="restore_waves",
    )(wave_order, returned)
    restored = restored.reshape(2, LOCAL, RQ * R5, 2, waves)
    return restored.transpose(0, 3, 1, 2, 4)


def solution(mesh):
    placed = (
        P(None, None, "lev", "wave", None),
        P(),
        P(),
        P(),
        P("wave", None, None),
        P(),
        P(),
        P(),
        P(),
        P(),
        P(),
    )
    return jax.shard_map(
        local,
        mesh=mesh,
        in_specs=placed,
        out_specs=P(None, None, "lev", "wave", None),
        check_vma=False,
    )
```

time: 174 us -> 159 us (0.914)
  waiting for transfers between devices: 50.4 us -> 15.1 us
  local copies, waits for them, and re-layouts: 2.41 us -> 23.5 us
  Pallas kernels: 40.1 us -> 27.1 us
  other arithmetic: 2.39 us -> 14.5 us
    all_to_all x1, waiting for transfers between devices: 50.4 us -> 15.1 us  [local(): lax.all_to_all(sent, ('wave', 'lev'), split_axis=0, concat_axis=0, tiled=...]
    mul x0 -> x6, local copies, waits for them, and re-layouts: none -> 21.3 us  [the longest x2 14 us: local(): wide_first = (fold * twin.reshape(1, 1, 2, 1, 1, 2)).reshape(4 * X, XW)]
    mul x0 -> x2, other arithmetic: none -> 12.8 us  [the longest x1 8.13 us: local(): wide_first = (fold * twin.reshape(1, 1, 2, 1, 1, 2)).reshape(4 * X, XW)]
    pallas_call x1, Pallas kernels: 23.6 us -> 15.9 us  [local(): pl.pallas_call(spectral_kernel, in_specs=[smem] + [vmem] * 4 + [hbm], out...]
    pallas_call x1, Pallas kernels: 10.3 us -> 6.83 us  [local(): pl.pallas_call(select_kernel, in_specs=[vmem, hbm], out_specs=hbm, out_sh...]
    pallas_call x1, Pallas kernels: 6.19 us -> 4.36 us  [local(): pl.pallas_call(restore_kernel, in_specs=[vmem] * 2, out_specs=hbm, out_sh...]
  transfers between devices with their start and end apart: 1 -> 1, of which waited for: 1 -> 1; matrix products, arithmetic and copies ran while one was open for 2% -> 25% of each run, Pallas kernels for 0% -> 0%
where the time goes in v2:
time: 159 us; the launch traced here: 158 us
  blocking collectives  60.6 us (38%)
  Pallas kernels  27.1 us (17%)
  local copies, waits for them, and re-layouts  23.5 us (15%)
  starting transfers between devices  15.7 us (10%)
  waiting for transfers between devices  15.1 us (9%)
  other arithmetic  14.5 us (9%)
    all_to_all x1, blocking collectives, local(): lax.all_to_all(solved, ('wave', 'lev'), split_axis=0, concat_axis=0, tile...  60.6 us
    pallas_call x1, Pallas kernels, local(): pl.pallas_call(spectral_kernel, in_specs=[smem] + [vmem] * 4 + [hbm], out...  15.9 us
    all_to_all x1, starting transfers between devices, local(): lax.all_to_all(sent, ('wave', 'lev'), split_axis=0, concat_axis=0, tiled=...  15.7 us
    all_to_all x1, waiting for transfers between devices, local(): lax.all_to_all(sent, ('wave', 'lev'), split_axis=0, concat_axis=0, tiled=...  15.1 us
    mul x2, local copies, waits for them, and re-layouts, local(): wide_first = (fold * twin.reshape(1, 1, 2, 1, 1, 2)).reshape(4 * X, XW)  14 us
    mul x1, other arithmetic, local(): wide_first = (fold * twin.reshape(1, 1, 2, 1, 1, 2)).reshape(4 * X, XW)  8.13 us
    mul x4, local copies, waits for them, and re-layouts, local(): wide_second = (spread * twin.reshape(1, 2, 1, 2)).reshape(XW, 2 * X)  7.32 us
    pallas_call x1, Pallas kernels, local(): pl.pallas_call(select_kernel, in_specs=[vmem, hbm], out_specs=hbm, out_sh...  6.83 us
  transfers between devices with their start and end apart: 1, of which 1 were waited for; matrix products, arithmetic and copies ran while one was open for 25% of the time, Pallas kernels for 0%

profile of v2, /device:TPU:1, one launch (start us, length us, event | category | flops | bytes accessed | tf_op | source)
XLA Modules:
  0.0 158.4 jit_solution(833548717730903871)
XLA Ops:
  0.0 0.0 copy-start
  0.0 6.8 %select_waves.1 = bf16[256,8,512]{2,1,0:T(8,128)(2,1)} custom-call(s32[640]{0:T(1024)} %wave_ref.3, bf16[36,20,2,640]{3,2,1,0:T(2,128)(2,1)} %bitcast.30), custom_call_target="tpu_custom_call" | custom-call | tf_op jit(solution)/shard_map/select_waves/pallas_call | solution.py:401
  6.8 15.7 %all-to-all-start = ((bf16[256,8,512]{2,1,0:T(8,128)(2,1)}), bf16[256,8,512]{2,1,0:T(8,128)(2,1)S(1)}, u32[]{:S(2)}, u32[]{:S(2)}) async-start(bf16[256,8,512]{2,1,0:T(8,128)(2,1)} %select_waves.1), calls=%async_computation | async-start | bytes 4194304 | tf_op jit(solution)/shard_map/all_to_all | solution.py:417
  22.5 0.8 copy.13
  23.4 0.0 copy-done
  23.4 1.0 fusion.13
  24.5 0.1 copy.16
  24.6 8.1 %broadcast_multiply_fusion = f32[2,72,2,4,36,2]{2,1,0,5,4,3:T(8,128)} fusion(f32[2,2]{0,1:T(2,128)S(1)} %compare_convert_fusion, f32[2,72,4,36]{1,0,3,2:T(2,128)S(1)} %copy.16), kind=kLoop, calls=%fused_computation | loop fusion | flops 82944 | bytes 414736 | tf_op jit(solution)/shard_map/mul | solution.py:380
  32.7 0.0 copy-start.2
  32.7 0.0 copy-start.3
  32.7 13.0 %mul.101 = f32[288,288]{0,1:T(8,128)S(1)} reshape(f32[2,72,2,4,36,2]{2,1,0,5,4,3:T(8,128)} %broadcast_multiply_fusion) | data formatting | bytes 663552 | tf_op jit(solution)/shard_map/mul | solution.py:380
  45.7 1.0 copy.19
  46.7 0.0 copy-done.2
  46.7 0.0 copy-done.3
  46.7 0.2 convolution_negate_fusion
  47.0 0.1 copy.17
  47.1 0.0 copy-start.6
  47.1 0.0 copy-start.1
  47.1 0.0 copy-start.7
  47.1 0.0 copy-start.4
  47.1 0.0 copy-start.5
  47.1 4.7 %broadcast_multiply_fusion.1 = f32[144,2,72,2]{1,0,3,2:T(8,128)} fusion(f32[2,2]{0,1:T(2,128)S(1)} %compare_convert_fusion, f32[144,72]{0,1:T(8,128)S(1)} %copy.17), kind=kLoop, calls=%fused_computation.1 | loop fusion | flops 41472 | bytes 207376 | tf_op jit(solution)/shard_map/mul | solution.py:384
  51.8 7.1 %mul.106 = f32[288,144]{0,1:T(8,128)S(1)} reshape(f32[144,2,72,2]{1,0,3,2:T(8,128)} %broadcast_multiply_fusion.1) | data formatting | bytes 331776 | tf_op jit(solution)/shard_map/mul | solution.py:384
  58.9 0.1 copy.18
  59.1 0.0 copy-done.6
  59.1 0.1 broadcast_in_dim.27
  59.2 0.1 reshape.152
  59.3 0.0 copy-done.1
  59.4 0.1 and_select_fusion.1
  59.4 0.0 copy-done.7
  59.4 0.2 fusion
  59.6 0.2 broadcast_in_dim.11
  59.8 0.2 reshape.146
  60.0 0.0 copy-done.4
  60.0 0.2 convert_element_type.87
  60.3 0.1 copy.12
  60.4 0.1 convert_element_type.89
  60.5 0.0 copy-done.5
  60.5 0.1 maximum_maximum_fusion
  60.7 0.1 copy.15
  60.8 0.1 pad_add_fusion.place_ref
  60.9 0.1 multiply_add_fusion.1
  61.1 0.1 multiply_add_fusion
  61.2 1.1 pad_maximum_fusion.wide_ref
  62.3 15.1 %all-to-all-done.r_ref = bf16[256,8,512]{2,1,0:T(8,128)(2,1)S(1)} async-done(((bf16[256,8,512]{2,1,0:T(8,128)(2,1)}), bf16[256,8,512]{2,1,0:T(8,128)(2,1)S(1)}, u32[]{:S(2)}, u32[]{:S(2)}) %all-to-all-start) | async-done | bytes 2097184 | tf_op jit(solution)/shard_map/all_to_all | solution.py:417
  77.3 15.9 %spectral_round.1 = bf16[256,8,512]{2,1,0:T(8,128)(2,1)S(1)} custom-call(s32[11]{0:T(128)S(1)} %pad_add_fusion.place_ref, bf16[256,8,512]{2,1,0:T(8,128)(2,1)S(1)} %all-to-all-done.r_ref, f32[13,640]{1,0:T(8,128)S(1)} %pad_maximum_fusion.4.rows_ref, f32[304,160]{1,0:T(8,128)S(1)} %pad_maximum_fusion.1.vert_ref, f32[576,288]{1,0:T(8,128)S(1)} %pad_maximum_fusion.wide_ref, ...), custom_call_target="tpu_custom_call" | custom-call | tf_op jit(solution)/shard_map/spectral_round/pallas_call | solution.py:418
  93.3 60.6 %all_to_all.10.r_ref = bf16[256,8,512]{2,1,0:T(8,128)(2,1)S(1)} all-to-all(bf16[256,8,512]{2,1,0:T(8,128)(2,1)S(1)} %spectral_round.1), channel_id=1, replica_groups=mesh['wave'=64,'lev'=4] {'wave','lev'}, dimensions={0} | all-to-all | bytes 4194304 | tf_op jit(solution)/shard_map/all_to_all | solution.py:436
  153.9 4.4 %restore_waves.1 = bf16[36,20,2,640]{3,2,1,0:T(2,128)(2,1)} custom-call(s32[640]{0:T(1024)S(1)} %copy-done.1, bf16[256,8,512]{2,1,0:T(8,128)(2,1)S(1)} %all_to_all.10.r_ref), custom_call_target="tpu_custom_call" | custom-call | tf_op jit(solution)/shard_map/restore_waves/pallas_call | solution.py:437
  (22 shorter events, 0.2 us)
Async XLA Ops:
  0.0 23.4 %copy-start = (f32[72,72]{1,0:T(8,128)S(1)}, f32[72,72]{1,0:T(8,128)}, u32[]{:S(2)}) copy-start(f32[72,72]{1,0:T(8,128)} %param.17) | copy-start | bytes 62212
  6.8 70.5 %all-to-all-start = ((bf16[256,8,512]{2,1,0:T(8,128)(2,1)}), bf16[256,8,512]{2,1,0:T(8,128)(2,1)S(1)}, u32[]{:S(2)}, u32[]{:S(2)}) async-start(bf16[256,8,512]{2,1,0:T(8,128)(2,1)} %select_waves.1), calls=%async_computation | async-start | bytes 4194304 | tf_op jit(solution)/shard_map/all_to_all | solution.py:417
  32.7 14.0 %copy-start.2 = (f32[72,72]{1,0:T(8,128)S(1)}, f32[72,72]{1,0:T(8,128)}, u32[]{:S(2)}) copy-start(f32[72,72]{1,0:T(8,128)} %param.18) | copy-start | bytes 62212
  32.7 14.0 %copy-start.3 = (f32[72,72]{1,0:T(8,128)S(1)}, f32[72,72]{1,0:T(8,128)}, u32[]{:S(2)}) copy-start(f32[72,72]{1,0:T(8,128)} %param.20) | copy-start | bytes 62212
  47.1 12.0 %copy-start.6 = (f32[72]{0:T(128)S(1)}, f32[72]{0:T(128)}, u32[]{:S(2)}) copy-start(f32[72]{0:T(128)} %param.21) | copy-start | bytes 868
  47.1 12.3 %copy-start.1 = (s32[640]{0:T(1024)S(1)}, s32[640]{0:T(1024)}, u32[]{:S(2)}) copy-start(s32[640]{0:T(1024)} %wave_ref.3) | copy-start | bytes 7684
  47.1 12.3 %copy-start.7 = (s32[64,64]{1,0:T(8,128)S(1)}, s32[64,64]{1,0:T(8,128)}, u32[]{:S(2)}) copy-start(s32[64,64]{1,0:T(8,128)} %param.14) | copy-start | bytes 49156
  47.1 12.9 %copy-start.4 = (s32[1280]{0:T(1024)S(1)}, s32[1280]{0:T(1024)}, u32[]{:S(2)}) copy-start(s32[1280]{0:T(1024)} %param.12) | copy-start | bytes 15364
  47.1 13.4 %copy-start.5 = (f32[640]{0:T(1024)S(1)}, f32[640]{0:T(1024)}, u32[]{:S(2)}) copy-start(f32[640]{0:T(1024)} %param.16) | copy-start | bytes 7684

commit v3 on v2

--- a/solution.py
+++ b/solution.py
@@ -7,7 +7,6 @@
 
 RQ, R5 = 4, 5
 ROWS = 8
-PITCH = 40
 LANES = 512
 LEV = 4
 LOCAL = 18
@@ -23,7 +22,7 @@
 TOTAL = 2 * XW + XP
 WHOLE = ((0, 1), (3, 4), (5, 6), (8, 9))
 SHARED = (2, 7)
-CUTS = 2
+CUTS = 4
 NT = (((1,), (1,)), ((), ()))
 TN = (((0,), (0,)), ((), ()))
 NN = (((1,), (0,)), ((), ()))
@@ -52,27 +51,24 @@
 
 def put_block(scr, block_ref):
     width = scr.shape[2]
-    for w in range(block_ref.shape[0] // LEV):
-        for t in range(scr.shape[0]):
-            part = block_ref[w * LEV : (w + 1) * LEV, :, t * width : (t + 1) * width].astype(F32)
-            scr[t, w * PITCH : w * PITCH + LEV * ROWS, :] = part.reshape(LEV * ROWS, width)
+    for t in range(scr.shape[0]):
+        part = block_ref[:, :, t * width : (t + 1) * width].astype(F32)
+        scr[t] = part.reshape(scr.shape[1:])
 
 
 def get_block(scr, out_ref, first, last):
     width = scr.shape[2]
-    for w in range(first, last):
-        for t in range(scr.shape[0]):
-            part = scr[t, w * PITCH : w * PITCH + LEV * ROWS, :].reshape(LEV, ROWS, width)
-            out_ref[w * LEV : (w + 1) * LEV, :, t * width : (t + 1) * width] = part.astype(BF16)
+    for t in range(scr.shape[0]):
+        part = scr[t, first * ROWS : last * ROWS, :].reshape(last - first, ROWS, width)
+        out_ref[first:last, :, t * width : (t + 1) * width] = part.astype(BF16)
 
 
 def send_block(scr, out_buf, out_hbm, out_sem):
-    peers = out_buf.shape[0] // LEV
-    step = peers // CUTS
+    step = out_buf.shape[0] // CUTS
     stores = []
     for cut in range(CUTS):
         get_block(scr, out_buf, cut * step, (cut + 1) * step)
-        part = pl.ds(cut * step * LEV, step * LEV)
+        part = pl.ds(cut * step, step)
         stores.append(pltpu.make_async_copy(out_buf.at[part], out_hbm.at[part], out_sem.at[cut]))
         stores[-1].start()
     for store in stores:
@@ -141,8 +137,8 @@
         def put(peer, tile, values):
             for t in range(values.shape[1] // 128):
                 side, lane = (tile + t) // 4, (tile + t) % 4
-                start = peer * ROWS + rq * 2 + side
-                scr[lane, pl.ds(start, peers, stride=PITCH), :] = values[:, t * 128 : (t + 1) * 128]
+                start = peer * peers * ROWS + rq * 2 + side
+                scr[lane, pl.ds(start, peers, stride=ROWS), :] = values[:, t * 128 : (t + 1) * 128]
 
         for peer in range(LEV):
             for i, kk in enumerate(WHOLE[peer]):
@@ -155,11 +151,6 @@
     send_block(scr, out_buf, out_hbm, out_sem)
 
 
-def split(values):
-    high = values.astype(BF16)
-    return high, (values - high.astype(F32)).astype(BF16)
-
-
 def slots_of(p):
     for i in range(2):
         yield i * SIDE, PAIR, i * XW + p * PAIR
@@ -167,17 +158,12 @@
 
 
 def solve(state_low, factor, first, second, keep, modes):
-    first_high, first_low = first
-    second_high, second_low = second
     size = modes.shape[0]
-    mixed = dot(first_high, state_low, NN) + dot(first_low, state_low, NN)
+    mixed = dot(first, jnp.concatenate([state_low, state_low], axis=0), NN)
     modal = (mixed[:size] + factor * mixed[size:]) / (1.0 + factor * modes)
-    modal_high, modal_low = split(modal)
-    new = (
-        dot(second_high, modal_high, NN)
-        + dot(second_high, modal_low, NN)
-        + dot(second_low, modal_high, NN)
-    )
+    high = modal.astype(BF16).astype(F32)
+    stacked = jnp.concatenate([high, modal - high, high], axis=0).astype(BF16)
+    new = dot(second, stacked, NN)
     return (new + keep * state_low.astype(F32)).astype(BF16)
 
 
@@ -204,7 +190,7 @@
             part = jnp.concatenate(
                 [
                     jnp.concatenate(
-                        [get_rows(scr, p * ROWS + 2 * rq + side, peers, PITCH) for side in range(2)],
+                        [get_rows(scr, p * peers * ROWS + 2 * rq + side, peers, ROWS) for side in range(2)],
                         axis=1,
                     )
                     for rq in (2 * pair, 2 * pair + 1)
@@ -225,17 +211,14 @@
         sym_scr[:, block * hb : (block + 1) * hb] = ((north + south) * weight).astype(BF16)
         anti_scr[:, block * hb : (block + 1) * hb] = ((north - south) * weight).astype(BF16)
 
-    wide = (
-        split(wide_ref[:XW, :]),
-        split(wide_ref[XW:, : 2 * X]),
-        wide_ref[XW:, 2 * X : 2 * X + 1],
-        wide_ref[XW : XW + 2 * X, 2 * X + 1 : 2 * X + 2],
-    )
-    narrow = (
-        split(vert_ref[: 2 * X, :]),
-        split(vert_ref[2 * X :, :X]),
-        vert_ref[2 * X :, X : X + 1],
-        vert_ref[2 * X : 3 * X, X + 1 : X + 2],
+    wide, narrow = (
+        (
+            ref[: 2 * size, : 2 * span_in].astype(BF16),
+            ref[2 * size :, : 3 * size].astype(BF16),
+            ref[2 * size :, 3 * size : 3 * size + 1],
+            ref[2 * size : 3 * size, 3 * size + 1 : 3 * size + 2],
+        )
+        for ref, size, span_in in ((wide_ref, 2 * X, XW), (vert_ref, X, XP))
     )
     degree = lax.broadcasted_iota(jnp.int32, (1, waves), 1)
     factor = (degree * (degree + 1)).astype(F32) / float(waves * (waves + 1))
@@ -268,10 +251,10 @@
             turned = band_scr[p, :, pair * span : (pair + 1) * span].T
             for i in range(2):
                 for side in range(2):
-                    start = p * ROWS + (2 * pair + i) * 2 + side
+                    start = p * peers * ROWS + (2 * pair + i) * 2 + side
                     piece = turned[i * peers : (i + 1) * peers, side * LANES : (side + 1) * LANES]
-                    put_rows(scr, start, peers, PITCH, piece)
-    get_block(scr, out_ref, 0, peers)
+                    put_rows(scr, start, peers, ROWS, piece)
+    get_block(scr, out_ref, 0, out_ref.shape[0])
 
 
 def restore_kernel(wave_ref, r_ref, out_hbm, scr, out_buf, out_sem):
@@ -286,8 +269,8 @@
         def get(peer, tile, tiles):
             values = []
             for t in range(tile, tile + tiles):
-                start = peer * ROWS + rq * 2 + t // 4
-                values.append(scr[t % 4, pl.ds(start, peers, stride=PITCH), :])
+                start = peer * peers * ROWS + rq * 2 + t // 4
+                values.append(scr[t % 4, pl.ds(start, peers, stride=ROWS), :])
             return jnp.concatenate(values, axis=1)
 
         parts = {}
@@ -316,6 +299,21 @@
         store.wait()
 
 
+def stack_terms(first, second, keep, modes):
+    def parts(matrix):
+        high = lax.reduce_precision(matrix, 8, 7)
+        return high, matrix - high
+
+    first_high, first_low = parts(first)
+    second_high, second_low = parts(second)
+    rows, size = second.shape
+    column = jnp.pad(modes, (0, rows - size))[:, None]
+    top = jnp.concatenate([first_high, first_low], axis=1)
+    bottom = jnp.concatenate([second_high, second_high, second_low, keep, column], axis=1)
+    bottom = jnp.pad(bottom, ((0, 0), (0, top.shape[1] - bottom.shape[1])))
+    return jnp.concatenate([top, bottom], axis=0)
+
+
 def local(
     fourier,
     lat_order,
@@ -364,10 +362,7 @@
     second = jnp.pad(second, gap).reshape(XP, X)
     place = jnp.arange(XP, dtype=jnp.int32) % UNIT
     keep = ((place >= LOCAL) & (place < FL)).astype(F32)[:, None]
-    column = jnp.arange(XP, dtype=jnp.int32)[None, :]
-    second = jnp.pad(second, ((0, 0), (0, XP - X))) + keep * (column == X).astype(F32)
-    second = second + jnp.pad(modes, (0, XP - X))[:, None] * (column == X + 1).astype(F32)
-    vert = jnp.concatenate([first, second], axis=0)
+    vert = stack_terms(first, second, keep, modes)
 
     twin = jnp.eye(2, dtype=F32)
     none = jnp.zeros((X, LEV, LOCAL), F32)
@@ -384,11 +379,7 @@
     wide_second = (spread * twin.reshape(1, 2, 1, 2)).reshape(XW, 2 * X)
     place = (jnp.arange(XW, dtype=jnp.int32) % PAIR) // 2
     keep = (place >= LOCAL).astype(F32)[:, None]
-    column = jnp.arange(XW, dtype=jnp.int32)[None, :]
-    wide_second = jnp.pad(wide_second, ((0, 0), (0, XW - 2 * X))) + keep * (column == 2 * X).astype(F32)
-    modes_twin = jnp.pad(jnp.repeat(modes, 2), (0, XW - 2 * X))[:, None]
-    wide_second = wide_second + modes_twin * (column == 2 * X + 1).astype(F32)
-    wide_vert = jnp.concatenate([wide_first, wide_second], axis=0)
+    wide_vert = stack_terms(wide_first, wide_second, keep, jnp.repeat(modes, 2))
 
     vmem = pl.BlockSpec(memory_space=pltpu.VMEM)
     smem = pl.BlockSpec(memory_space=pltpu.SMEM)
@@ -396,7 +387,7 @@
     peers = count * LEV
     rowed = (FL, RQ * R5, 2, waves)
     block = jax.ShapeDtypeStruct((peers, ROWS, LANES), BF16)
-    block_scratch = pltpu.VMEM((LANES // 128, count * PITCH, 128), F32)
+    block_scratch = pltpu.VMEM((LANES // 128, peers * ROWS, 128), F32)
 
     sent = pl.pallas_call(
         select_kernel,
@@ -414,7 +405,7 @@
         compiler_params=params(60),
         name="select_waves",
     )(wave_order, fourier.transpose(0, 2, 3, 1, 4).reshape(rowed))
-    arrived = lax.all_to_all(sent, ("wave", "lev"), split_axis=0, concat_axis=0, tiled=True)
+    arrived = lax.all_to_all(sent, ("lev", "wave"), split_axis=0, concat_axis=0, tiled=True)
     solved = pl.pallas_call(
         spectral_kernel,
         in_specs=[smem] + [vmem] * 4 + [hbm],
@@ -433,7 +424,7 @@
         compiler_params=params(46),
         name="spectral_round",
     )(places, arrived, rows_in, vert, wide_vert, legendre)
-    returned = lax.all_to_all(solved, ("wave", "lev"), split_axis=0, concat_axis=0, tiled=True)
+    returned = lax.all_to_all(solved, ("lev", "wave"), split_axis=0, concat_axis=0, tiled=True)
     restored = pl.pallas_call(
         restore_kernel,
         in_specs=[vmem] * 2,

time: 159 us -> 162 us (1.019)
  waiting for transfers between devices: 15.1 us -> 4.82 us
  other arithmetic: 14.5 us -> 21.2 us
  local copies, waits for them, and re-layouts: 23.5 us -> 29.2 us
  blocking collectives: 60.6 us -> 63.5 us
    all_to_all x1, waiting for transfers between devices: 15.1 us -> 4.82 us  [local(): lax.all_to_all(sent, ('lev', 'wave'), split_axis=0, concat_axis=0, tiled=...]
    all_to_all x1, blocking collectives: 60.6 us -> 63.5 us  [local(): lax.all_to_all(solved, ('lev', 'wave'), split_axis=0, concat_axis=0, tile...]
    reduce_precision x0 -> x3, other arithmetic: none -> 2.03 us  [parts(): high = lax.reduce_precision(matrix, 8, 7)]
    sub x0 -> x2, other arithmetic: none -> 1.93 us  [parts(): return (high, matrix - high)]
  transfers between devices with their start and end apart: 1 -> 1, of which waited for: 1 -> 1; matrix products, arithmetic and copies ran while one was open for 25% -> 31% of each run, Pallas kernels for 0% -> 0%
where the time goes in v3:
time: 162 us
  blocking collectives  63.5 us (39%)
  local copies, waits for them, and re-layouts  29.2 us (18%)
  Pallas kernels  26 us (16%)
  other arithmetic  21.2 us (13%)
  starting transfers between devices  15.7 us (10%)
  waiting for transfers between devices  4.82 us (3%)
    all_to_all x1, blocking collectives, local(): lax.all_to_all(solved, ('lev', 'wave'), split_axis=0, concat_axis=0, tile...  63.5 us
    all_to_all x1, starting transfers between devices, local(): lax.all_to_all(sent, ('lev', 'wave'), split_axis=0, concat_axis=0, tiled=...  15.7 us
    pallas_call x1, Pallas kernels, local(): pl.pallas_call(spectral_kernel, in_specs=[smem] + [vmem] * 4 + [hbm], out...  15 us
    mul x2, local copies, waits for them, and re-layouts, local(): wide_first = (fold * twin.reshape(1, 1, 2, 1, 1, 2)).reshape(4 * X, XW)  14.2 us
    mul x1, other arithmetic, local(): wide_first = (fold * twin.reshape(1, 1, 2, 1, 1, 2)).reshape(4 * X, XW)  8.07 us
    mul x4, local copies, waits for them, and re-layouts, local(): wide_second = (spread * twin.reshape(1, 2, 1, 2)).reshape(XW, 2 * X)  7.9 us
    pallas_call x1, Pallas kernels, local(): pl.pallas_call(select_kernel, in_specs=[vmem, hbm], out_specs=hbm, out_sh...  6.74 us
    all_to_all x1, waiting for transfers between devices, local(): lax.all_to_all(sent, ('lev', 'wave'), split_axis=0, concat_axis=0, tiled=...  4.82 us
  transfers between devices with their start and end apart: 1, of which 1 were waited for; matrix products, arithmetic and copies ran while one was open for 31% of the time, Pallas kernels for 0%

profile of v3, /device:TPU:1, one launch (start us, length us, event | category | flops | bytes accessed | tf_op | source)
XLA Modules:
  0.0 161.7 jit_solution(16425411169551854166)
XLA Ops:
  0.0 0.0 copy-start
  0.0 6.7 %select_waves.1 = bf16[256,8,512]{2,1,0:T(8,128)(2,1)} custom-call(s32[640]{0:T(1024)} %wave_ref.3, bf16[36,20,2,640]{3,2,1,0:T(2,128)(2,1)} %bitcast.35), custom_call_target="tpu_custom_call" | custom-call | tf_op jit(solution)/shard_map/select_waves/pallas_call | solution.py:392
  6.8 0.0 copy-start.4
  6.8 15.7 %all-to-all-start = ((bf16[256,8,512]{2,1,0:T(8,128)(2,1)}), bf16[256,8,512]{2,1,0:T(8,128)(2,1)S(1)}, u32[]{:S(2)}, u32[]{:S(2)}) async-start(bf16[256,8,512]{2,1,0:T(8,128)(2,1)} %select_waves.1), calls=%async_computation | async-start | bytes 4194304 | tf_op jit(solution)/shard_map/all_to_all | solution.py:408
  22.4 0.0 copy-done
  22.4 0.0 copy-done.4
  22.5 0.2 convolution_negate_fusion
  22.7 0.1 copy.35
  22.8 4.7 %broadcast_multiply_fusion.1 = f32[144,2,72,2]{1,0,3,2:T(8,128)} fusion(f32[2,2]{0,1:T(2,128)S(1)} %compare_convert_fusion, f32[144,72]{0,1:T(8,128)S(1)} %copy.35), kind=kLoop, calls=%fused_computation.1 | loop fusion | flops 41472 | bytes 207376 | tf_op jit(solution)/shard_map/mul | solution.py:379
  27.5 0.0 copy-start.8
  27.5 0.0 copy-start.3
  27.5 0.0 copy-start.5
  27.5 6.9 %mul.48 = f32[288,144]{0,1:T(8,128)S(1)} reshape(f32[144,2,72,2]{1,0,3,2:T(8,128)} %broadcast_multiply_fusion.1) | data formatting | bytes 331776 | tf_op jit(solution)/shard_map/mul | solution.py:379
  34.5 0.9 copy.36
  35.4 0.1 copy.38
  35.5 0.6 pad.22
  36.1 0.0 copy-done.8
  36.2 0.1 broadcast_in_dim.30
  36.2 0.1 reshape.190
  36.4 0.1 broadcast_in_dim.32
  36.5 0.0 copy-done.3
  36.5 0.1 copy.26
  36.6 0.0 copy-done.5
  36.6 0.3 fusion.20
  36.9 0.1 copy.32
  37.0 8.1 %broadcast_multiply_fusion = f32[2,72,2,4,36,2]{2,1,0,5,4,3:T(8,128)} fusion(f32[2,2]{0,1:T(2,128)S(1)} %compare_convert_fusion, f32[2,72,4,36]{1,0,3,2:T(2,128)S(1)} %copy.32), kind=kLoop, calls=%fused_computation | loop fusion | flops 82944 | bytes 414736 | tf_op jit(solution)/shard_map/mul | solution.py:375
  45.1 0.0 copy-start.2
  45.1 0.0 copy-start.9
  45.1 13.2 %mul.43 = f32[288,288]{0,1:T(8,128)S(1)} reshape(f32[2,72,2,4,36,2]{2,1,0,5,4,3:T(8,128)} %broadcast_multiply_fusion) | data formatting | bytes 663552 | tf_op jit(solution)/shard_map/mul | solution.py:375
  58.3 0.0 copy-start.6
  58.3 0.0 copy-start.7
  58.3 1.0 copy.33
  59.3 0.1 copy.31
  59.4 0.1 maximum_maximum_fusion
  59.6 0.8 copy.28
  60.3 0.0 copy-done.2
  60.3 0.6 and_select_fusion
  60.9 0.0 copy-done.9
  60.9 0.2 fusion.15
  61.1 0.2 broadcast_in_dim.26
  61.3 0.8 reshape.184
  62.1 0.0 copy-done.6
  62.1 0.2 convert_element_type.61
  62.4 0.1 copy.25
  62.5 0.1 convert_element_type.63
  62.6 0.0 copy-done.7
  62.6 0.6 broadcast_in_dim.27
  63.2 1.0 sub.26
  64.2 0.8 fusion.5
  65.0 1.4 concatenate.55
  66.4 0.9 bitcast_subtract_fusion
  67.3 0.2 concatenate.50
  67.5 0.7 pad_add_fusion.place_ref
  68.2 0.8 pad_maximum_fusion.2.rows_ref
  69.0 0.9 fusion.19
  69.9 0.1 select_maximum_fusion.1.vert_ref
  70.0 1.1 fusion.18
  71.1 1.3 select_maximum_fusion.wide_ref
  72.4 4.8 %all-to-all-done.r_ref = bf16[256,8,512]{2,1,0:T(8,128)(2,1)S(1)} async-done(((bf16[256,8,512]{2,1,0:T(8,128)(2,1)}), bf16[256,8,512]{2,1,0:T(8,128)(2,1)S(1)}, u32[]{:S(2)}, u32[]{:S(2)}) %all-to-all-start) | async-done | bytes 2097184 | tf_op jit(solution)/shard_map/all_to_all | solution.py:408
  77.3 0.0 copy-start.1
  77.3 1.4 copy-done.1
  78.6 15.0 %spectral_round.1 = bf16[256,8,512]{2,1,0:T(8,128)(2,1)S(1)} custom-call(s32[11]{0:T(128)S(1)} %pad_add_fusion.place_ref, bf16[256,8,512]{2,1,0:T(8,128)(2,1)S(1)} %all-to-all-done.r_ref, f32[13,640]{1,0:T(8,128)S(1)} %pad_maximum_fusion.2.rows_ref, f32[304,320]{1,0:T(8,128)S(1)} %select_maximum_fusion.1.vert_ref, f32[576,576]{1,0:T(8,128)S(1)} %copy-done.1, ...), custom_call_target="tpu_custom_call" | custom-call | tf_op jit(solution)/shard_map/spectral_round/pallas_call | solution.py:409
  93.6 63.5 %all_to_all.10.r_ref = bf16[256,8,512]{2,1,0:T(8,128)(2,1)S(1)} all-to-all(bf16[256,8,512]{2,1,0:T(8,128)(2,1)S(1)} %spectral_round.1), channel_id=1, replica_groups=mesh['wave'=64,'lev'=4] {'lev','wave'}, dimensions={0} | all-to-all | bytes 4194304 | tf_op jit(solution)/shard_map/all_to_all | solution.py:427
  157.1 4.3 %restore_waves.1 = bf16[36,20,2,640]{3,2,1,0:T(2,128)(2,1)} custom-call(s32[640]{0:T(1024)S(1)} %copy-done.2, bf16[256,8,512]{2,1,0:T(8,128)(2,1)S(1)} %all_to_all.10.r_ref), custom_call_target="tpu_custom_call" | custom-call | tf_op jit(solution)/shard_map/restore_waves/pallas_call | solution.py:428
  (16 shorter events, 0.2 us)
Async XLA Ops:
  0.0 22.4 %copy-start = (f32[72,72]{1,0:T(8,128)S(1)}, f32[72,72]{1,0:T(8,128)}, u32[]{:S(2)}) copy-start(f32[72,72]{1,0:T(8,128)} %param.20) | copy-start | bytes 62212
  6.8 15.7 %copy-start.4 = (f32[72,72]{1,0:T(8,128)S(1)}, f32[72,72]{1,0:T(8,128)}, u32[]{:S(2)}) copy-start(f32[72,72]{1,0:T(8,128)} %param.18) | copy-start | bytes 62212
  6.8 70.5 %all-to-all-start = ((bf16[256,8,512]{2,1,0:T(8,128)(2,1)}), bf16[256,8,512]{2,1,0:T(8,128)(2,1)S(1)}, u32[]{:S(2)}, u32[]{:S(2)}) async-start(bf16[256,8,512]{2,1,0:T(8,128)(2,1)} %select_waves.1), calls=%async_computation | async-start | bytes 4194304 | tf_op jit(solution)/shard_map/all_to_all | solution.py:408
  27.5 8.6 %copy-start.8 = (f32[72]{0:T(128)S(1)}, f32[72]{0:T(128)}, u32[]{:S(2)}) copy-start(f32[72]{0:T(128)} %param.21) | copy-start | bytes 868
  27.5 9.0 %copy-start.3 = (f32[72,72]{1,0:T(8,128)S(1)}, f32[72,72]{1,0:T(8,128)}, u32[]{:S(2)}) copy-start(f32[72,72]{1,0:T(8,128)} %param.19) | copy-start | bytes 62212
  27.5 9.1 %copy-start.5 = (f32[72,72]{1,0:T(8,128)S(1)}, f32[72,72]{1,0:T(8,128)}, u32[]{:S(2)}) copy-start(f32[72,72]{1,0:T(8,128)} %param.17) | copy-start | bytes 62212
  45.1 15.2 %copy-start.2 = (s32[640]{0:T(1024)S(1)}, s32[640]{0:T(1024)}, u32[]{:S(2)}) copy-start(s32[640]{0:T(1024)} %wave_ref.3) | copy-start | bytes 7684
  45.1 15.8 %copy-start.9 = (s32[64,64]{1,0:T(8,128)S(1)}, s32[64,64]{1,0:T(8,128)}, u32[]{:S(2)}) copy-start(s32[64,64]{1,0:T(8,128)} %param.14) | copy-start | bytes 49156
  58.3 3.8 %copy-start.6 = (s32[1280]{0:T(1024)S(1)}, s32[1280]{0:T(1024)}, u32[]{:S(2)}) copy-start(s32[1280]{0:T(1024)} %param.12) | copy-start | bytes 15364
  58.3 4.3 %copy-start.7 = (f32[640]{0:T(1024)S(1)}, f32[640]{0:T(1024)}, u32[]{:S(2)}) copy-start(f32[640]{0:T(1024)} %param.16) | copy-start | bytes 7684
  77.3 1.4 copy-start.1

commit v4 on v3

--- a/solution.py
+++ b/solution.py
@@ -364,19 +364,27 @@
     keep = ((place >= LOCAL) & (place < FL)).astype(F32)[:, None]
     vert = stack_terms(first, second, keep, modes)
 
-    twin = jnp.eye(2, dtype=F32)
+    def twin(matrix):
+        rows, columns = matrix.shape
+        down = jnp.arange(2 * rows, dtype=jnp.int32)[:, None]
+        across = jnp.arange(2 * columns, dtype=jnp.int32)[None, :]
+        left = (down // 2 == jnp.arange(rows, dtype=jnp.int32)[None, :]).astype(F32)
+        right = (across // 2 == jnp.arange(columns, dtype=jnp.int32)[:, None]).astype(F32)
+        spread = jnp.dot(jnp.dot(left, matrix, precision=high), right, precision=high)
+        return jnp.where(down % 2 == across % 2, spread, 0.0)
+
     none = jnp.zeros((X, LEV, LOCAL), F32)
     fold = jnp.stack(
         [
             jnp.concatenate([einv.reshape(X, LEV, LOCAL), none], axis=2),
             jnp.concatenate([none, einv_link.reshape(X, LEV, LOCAL)], axis=2),
         ]
-    ).reshape(2, X, 1, LEV, FL, 1)
-    wide_first = (fold * twin.reshape(1, 1, 2, 1, 1, 2)).reshape(4 * X, XW)
+    ).reshape(2 * X, 2 * X)
+    wide_first = twin(fold)
     spread = jnp.concatenate(
         [evec.reshape(LEV, LOCAL, X), -heat_evec.reshape(LEV, LOCAL, X)], axis=1
-    ).reshape(X * 2, 1, X, 1)
-    wide_second = (spread * twin.reshape(1, 2, 1, 2)).reshape(XW, 2 * X)
+    ).reshape(2 * X, X)
+    wide_second = twin(spread)
     place = (jnp.arange(XW, dtype=jnp.int32) % PAIR) // 2
     keep = (place >= LOCAL).astype(F32)[:, None]
     wide_vert = stack_terms(wide_first, wide_second, keep, jnp.repeat(modes, 2))

time: 162 us -> 158 us (0.975)
  waiting for transfers between devices: 4.82 us -> 43.1 us
  local copies, waits for them, and re-layouts: 29.2 us -> 6.75 us
  other arithmetic: 21.2 us -> 3.57 us
  blocking collectives: 63.5 us -> 59.2 us
    all_to_all x1, waiting for transfers between devices: 4.82 us -> 43.1 us  [local(): lax.all_to_all(sent, ('lev', 'wave'), split_axis=0, concat_axis=0, tiled=...]
    mul x6 -> x0, local copies, waits for them, and re-layouts: 22.1 us -> none  [the longest x2 14.2 us: local(): wide_first = (fold * twin.reshape(1, 1, 2, 1, 1, 2)).reshape(4 * X, XW)]
    mul x2 -> x0, other arithmetic: 12.7 us -> none  [the longest x1 8.07 us: local(): wide_first = (fold * twin.reshape(1, 1, 2, 1, 1, 2)).reshape(4 * X, XW)]
    all_to_all x1, blocking collectives: 63.5 us -> 59.2 us  [local(): lax.all_to_all(solved, ('lev', 'wave'), split_axis=0, concat_axis=0, tile...]
    sub x2 -> x1, other arithmetic: 1.93 us -> 0.01 us  [parts(): return (high, matrix - high)]
  transfers between devices with their start and end apart: 1 -> 1, of which waited for: 1 -> 1; matrix products, arithmetic and copies ran while one was open for 31% -> 7% of each run, Pallas kernels for 0% -> 0%
where the time goes in v4:
time: 158 us; the launch traced here: 157 us
  blocking collectives  59.2 us (37%)
  waiting for transfers between devices  43.1 us (27%)
  Pallas kernels  26 us (16%)
  starting transfers between devices  15.8 us (10%)
  local copies, waits for them, and re-layouts  6.75 us (4%)
  other arithmetic  3.57 us (2%)
  matrix products  2.26 us (1%)
    all_to_all x1, blocking collectives, local(): lax.all_to_all(solved, ('lev', 'wave'), split_axis=0, concat_axis=0, tile...  59.2 us
    all_to_all x1, waiting for transfers between devices, local(): lax.all_to_all(sent, ('lev', 'wave'), split_axis=0, concat_axis=0, tiled=...  43.1 us
    all_to_all x1, starting transfers between devices, local(): lax.all_to_all(sent, ('lev', 'wave'), split_axis=0, concat_axis=0, tiled=...  15.8 us
    pallas_call x1, Pallas kernels, local(): pl.pallas_call(spectral_kernel, in_specs=[smem] + [vmem] * 4 + [hbm], out...  15 us
    pallas_call x1, Pallas kernels, local(): pl.pallas_call(select_kernel, in_specs=[vmem, hbm], out_specs=hbm, out_sh...  6.72 us
    pallas_call x1, Pallas kernels, local(): pl.pallas_call(restore_kernel, in_specs=[vmem] * 2, out_specs=hbm, out_sh...  4.34 us
  transfers between devices with their start and end apart: 1, of which 1 were waited for; matrix products, arithmetic and copies ran while one was open for 7% of the time, Pallas kernels for 0%

profile of v4, /device:TPU:1, one launch (start us, length us, event | category | flops | bytes accessed | tf_op | source)
XLA Modules:
  0.0 157.4 jit_solution(9448837907474881524)
XLA Ops:
  0.0 0.0 copy-start
  0.0 6.7 %select_waves.1 = bf16[256,8,512]{2,1,0:T(8,128)(2,1)} custom-call(s32[640]{0:T(1024)} %wave_ref.3, bf16[36,20,2,640]{3,2,1,0:T(2,128)(2,1)} %bitcast.33), custom_call_target="tpu_custom_call" | custom-call | tf_op jit(solution)/shard_map/select_waves/pallas_call | solution.py:400
  6.7 0.0 copy-start.8
  6.7 0.0 copy-start.7
  6.8 0.0 copy-start.2
  6.8 0.0 copy-start.10
  6.8 0.0 copy-start.5
  6.8 15.8 %all-to-all-start = ((bf16[256,8,512]{2,1,0:T(8,128)(2,1)}), bf16[256,8,512]{2,1,0:T(8,128)(2,1)S(1)}, u32[]{:S(2)}, u32[]{:S(2)}) async-start(bf16[256,8,512]{2,1,0:T(8,128)(2,1)} %select_waves.1), calls=%async_computation | async-start | bytes 4194304 | tf_op jit(solution)/shard_map/all_to_all | solution.py:416
  22.6 0.0 copy-start.9
  22.6 0.0 copy-start.4
  22.7 0.0 copy-start.6
  22.7 0.0 copy-done.8
  22.7 0.0 copy-done.7
  22.7 0.2 convert_element_type.52
  23.0 0.1 copy.22
  23.1 0.1 convert_element_type.54
  23.2 0.0 copy-done.2
  23.2 0.1 and_select_fusion.2
  23.3 0.0 copy-done.10
  23.3 0.2 fusion.21
  23.5 0.2 broadcast_in_dim.42
  23.6 0.2 reshape.316
  23.8 0.0 copy-done.5
  23.9 0.0 copy-done
  23.9 0.2 convolution_negate_fusion
  24.1 0.0 copy-done.9
  24.2 0.1 copy.28
  24.3 0.0 copy-done.4
  24.3 0.1 copy.23
  24.4 0.0 copy-done.6
  24.4 0.3 fusion.32
  24.7 0.1 maximum_maximum_fusion
  24.8 0.8 copy.25
  25.6 0.1 broadcast_in_dim.48
  25.7 0.1 reshape.324
  25.8 0.8 broadcast_in_dim.50
  26.6 0.1 copy.29
  26.7 0.8 reshape.322
  27.6 0.2 concatenate.50
  27.8 0.8 fusion.9
  28.6 0.4 fusion
  29.0 0.3 reduce-precision_subtract_fusion.1
  29.4 1.4 concatenate.55
  30.8 0.0 copy-start.3
  30.8 0.1 pad_add_fusion.place_ref
  30.9 0.9 fusion.31
  31.9 0.1 select_maximum_fusion.1.vert_ref
  32.0 0.0 copy-done.3
  32.0 0.4 fusion.1
  32.4 0.5 fusion.30
  32.9 1.3 select_maximum_fusion.wide_ref
  34.2 43.1 %all-to-all-done.r_ref = bf16[256,8,512]{2,1,0:T(8,128)(2,1)S(1)} async-done(((bf16[256,8,512]{2,1,0:T(8,128)(2,1)}), bf16[256,8,512]{2,1,0:T(8,128)(2,1)S(1)}, u32[]{:S(2)}, u32[]{:S(2)}) %all-to-all-start) | async-done | bytes 2097184 | tf_op jit(solution)/shard_map/all_to_all | solution.py:416
  77.3 0.0 copy-start.1
  77.3 1.4 copy-done.1
  78.7 15.0 %spectral_round.1 = bf16[256,8,512]{2,1,0:T(8,128)(2,1)S(1)} custom-call(s32[11]{0:T(128)S(1)} %pad_add_fusion.place_ref, bf16[256,8,512]{2,1,0:T(8,128)(2,1)S(1)} %all-to-all-done.r_ref, f32[13,640]{1,0:T(8,128)S(1)} %pad_maximum_fusion.2.rows_ref, f32[304,320]{1,0:T(8,128)S(1)} %select_maximum_fusion.1.vert_ref, f32[576,576]{1,0:T(8,128)S(1)} %copy-done.1, ...), custom_call_target="tpu_custom_call" | custom-call | tf_op jit(solution)/shard_map/spectral_round/pallas_call | solution.py:417
  93.6 59.2 %all_to_all.10.r_ref = bf16[256,8,512]{2,1,0:T(8,128)(2,1)S(1)} all-to-all(bf16[256,8,512]{2,1,0:T(8,128)(2,1)S(1)} %spectral_round.1), channel_id=1, replica_groups=mesh['wave'=64,'lev'=4] {'lev','wave'}, dimensions={0} | all-to-all | bytes 4194304 | tf_op jit(solution)/shard_map/all_to_all | solution.py:435
  152.8 4.3 %restore_waves.1 = bf16[36,20,2,640]{3,2,1,0:T(2,128)(2,1)} custom-call(s32[640]{0:T(1024)S(1)} %copy-done.2, bf16[256,8,512]{2,1,0:T(8,128)(2,1)S(1)} %all_to_all.10.r_ref), custom_call_target="tpu_custom_call" | custom-call | tf_op jit(solution)/shard_map/restore_waves/pallas_call | solution.py:436
  (20 shorter events, 0.2 us)
Async XLA Ops:
  0.0 23.9 %copy-start = (f32[72,72]{1,0:T(8,128)S(1)}, f32[72,72]{1,0:T(8,128)}, u32[]{:S(2)}) copy-start(f32[72,72]{1,0:T(8,128)} %param.20) | copy-start | bytes 62212
  6.7 16.0 %copy-start.8 = (f32[640]{0:T(1024)S(1)}, f32[640]{0:T(1024)}, u32[]{:S(2)}) copy-start(f32[640]{0:T(1024)} %param.16) | copy-start | bytes 7684
  6.7 16.0 %copy-start.7 = (s32[1280]{0:T(1024)S(1)}, s32[1280]{0:T(1024)}, u32[]{:S(2)}) copy-start(s32[1280]{0:T(1024)} %param.12) | copy-start | bytes 15364
  6.8 16.4 %copy-start.2 = (s32[640]{0:T(1024)S(1)}, s32[640]{0:T(1024)}, u32[]{:S(2)}) copy-start(s32[640]{0:T(1024)} %wave_ref.3) | copy-start | bytes 7684
  6.8 16.5 %copy-start.10 = (s32[64,64]{1,0:T(8,128)S(1)}, s32[64,64]{1,0:T(8,128)}, u32[]{:S(2)}) copy-start(s32[64,64]{1,0:T(8,128)} %param.14) | copy-start | bytes 49156
  6.8 17.1 %copy-start.5 = (f32[72,72]{1,0:T(8,128)S(1)}, f32[72,72]{1,0:T(8,128)}, u32[]{:S(2)}) copy-start(f32[72,72]{1,0:T(8,128)} %param.18) | copy-start | bytes 62212
  6.8 70.5 %all-to-all-start = ((bf16[256,8,512]{2,1,0:T(8,128)(2,1)}), bf16[256,8,512]{2,1,0:T(8,128)(2,1)S(1)}, u32[]{:S(2)}, u32[]{:S(2)}) async-start(bf16[256,8,512]{2,1,0:T(8,128)(2,1)} %select_waves.1), calls=%async_computation | async-start | bytes 4194304 | tf_op jit(solution)/shard_map/all_to_all | solution.py:416
  22.6 1.5 copy-start.9
  22.6 1.6 %copy-start.4 = (f32[72,72]{1,0:T(8,128)S(1)}, f32[72,72]{1,0:T(8,128)}, u32[]{:S(2)}) copy-start(f32[72,72]{1,0:T(8,128)} %param.19) | copy-start | bytes 62212
  22.7 1.7 %copy-start.6 = (f32[72,72]{1,0:T(8,128)S(1)}, f32[72,72]{1,0:T(8,128)}, u32[]{:S(2)}) copy-start(f32[72,72]{1,0:T(8,128)} %param.17) | copy-start | bytes 62212
  30.8 1.1 copy-start.3
  77.3 1.4 copy-start.1

commit v5 on v4

--- a/solution.py
+++ b/solution.py
@@ -168,8 +168,8 @@
 
 
 def spectral_kernel(
-    place_ref, r_ref, rows_ref, vert_ref, wide_ref, leg_hbm, out_ref,
-    ot_scr, scr, lat_scr, sym_scr, anti_scr, band_scr, leg_buf, leg_sem,
+    place_ref, r_ref, rows_ref, vert_hbm, wide_hbm, leg_hbm, out_ref,
+    ot_scr, scr, lat_scr, sym_scr, anti_scr, band_scr, leg_buf, leg_sem, vert_ref, wide_ref, solve_sem,
 ):
     peers = r_ref.shape[0] // LEV
     half = ot_scr.shape[0] // 2
@@ -183,6 +183,12 @@
     for i, kk in enumerate(held):
         loads.append(pltpu.make_async_copy(leg_hbm.at[kk], leg_buf.at[i], leg_sem.at[i]))
         loads[-1].start()
+    solve_loads = [
+        pltpu.make_async_copy(vert_hbm, vert_ref, solve_sem.at[0]),
+        pltpu.make_async_copy(wide_hbm, wide_ref, solve_sem.at[1]),
+    ]
+    for load in solve_loads:
+        load.start()
     fill_lat_matrix(rows_ref, ot_scr)
     put_block(scr, r_ref)
     for p in range(LEV):
@@ -211,6 +217,8 @@
         sym_scr[:, block * hb : (block + 1) * hb] = ((north + south) * weight).astype(BF16)
         anti_scr[:, block * hb : (block + 1) * hb] = ((north - south) * weight).astype(BF16)
 
+    for load in solve_loads:
+        load.wait()
     wide, narrow = (
         (
             ref[: 2 * size, : 2 * span_in].astype(BF16),
@@ -416,7 +424,7 @@
     arrived = lax.all_to_all(sent, ("lev", "wave"), split_axis=0, concat_axis=0, tiled=True)
     solved = pl.pallas_call(
         spectral_kernel,
-        in_specs=[smem] + [vmem] * 4 + [hbm],
+        in_specs=[smem] + [vmem] * 2 + [hbm] * 3,
         out_specs=vmem,
         out_shape=block,
         scratch_shapes=[
@@ -428,6 +436,9 @@
             pltpu.VMEM((LEV, WIDE, RQ * count), F32),
             pltpu.VMEM((3,) + legendre.shape[1:], BF16),
             pltpu.SemaphoreType.DMA((3,)),
+            pltpu.VMEM(vert.shape, F32),
+            pltpu.VMEM(wide_vert.shape, F32),
+            pltpu.SemaphoreType.DMA((2,)),
         ],
         compiler_params=params(46),
         name="spectral_round",

time: 158 us -> 158 us (level)
  no operation moved by 1% of the time
where the time goes in v5:
time: 158 us
  blocking collectives  59.2 us (37%)
  waiting for transfers between devices  43.3 us (27%)
  Pallas kernels  26.7 us (17%)
  starting transfers between devices  15.7 us (10%)
  local copies, waits for them, and re-layouts  6.75 us (4%)
  other arithmetic  3.57 us (2%)
  matrix products  2.26 us (1%)
    all_to_all x1, blocking collectives, local(): lax.all_to_all(solved, ('lev', 'wave'), split_axis=0, concat_axis=0, tile...  59.2 us
    all_to_all x1, waiting for transfers between devices, local(): lax.all_to_all(sent, ('lev', 'wave'), split_axis=0, concat_axis=0, tiled=...  43.3 us
    all_to_all x1, starting transfers between devices, local(): lax.all_to_all(sent, ('lev', 'wave'), split_axis=0, concat_axis=0, tiled=...  15.7 us
    pallas_call x1, Pallas kernels, local(): pl.pallas_call(spectral_kernel, in_specs=[smem] + [vmem] * 2 + [hbm] * 3,...  15.6 us
    pallas_call x1, Pallas kernels, local(): pl.pallas_call(select_kernel, in_specs=[vmem, hbm], out_specs=hbm, out_sh...  6.72 us
    pallas_call x1, Pallas kernels, local(): pl.pallas_call(restore_kernel, in_specs=[vmem] * 2, out_specs=hbm, out_sh...  4.34 us
  transfers between devices with their start and end apart: 1, of which 1 were waited for; matrix products, arithmetic and copies ran while one was open for 7% of the time, Pallas kernels for 0%

profile of v5, /device:TPU:1, one launch (start us, length us, event | category | flops | bytes accessed | tf_op | source)
XLA Modules:
  0.0 158.0 jit_solution(9954491348726989888)
XLA Ops:
  0.0 0.0 copy-start
  0.0 6.7 %select_waves.1 = bf16[256,8,512]{2,1,0:T(8,128)(2,1)} custom-call(s32[640]{0:T(1024)} %wave_ref.3, bf16[36,20,2,640]{3,2,1,0:T(2,128)(2,1)} %bitcast.33), custom_call_target="tpu_custom_call" | custom-call | tf_op jit(solution)/shard_map/select_waves/pallas_call | solution.py:408
  6.7 0.0 copy-start.8
  6.7 0.0 copy-start.7
  6.8 0.0 copy-start.2
  6.8 0.0 copy-start.10
  6.8 0.0 copy-start.5
  6.8 15.7 %all-to-all-start = ((bf16[256,8,512]{2,1,0:T(8,128)(2,1)}), bf16[256,8,512]{2,1,0:T(8,128)(2,1)S(1)}, u32[]{:S(2)}, u32[]{:S(2)}) async-start(bf16[256,8,512]{2,1,0:T(8,128)(2,1)} %select_waves.1), calls=%async_computation | async-start | bytes 4194304 | tf_op jit(solution)/shard_map/all_to_all | solution.py:424
  22.5 0.0 copy-start.9
  22.5 0.0 copy-start.4
  22.5 0.0 copy-start.6
  22.5 0.0 copy-done.8
  22.5 0.0 copy-done.7
  22.5 0.2 convert_element_type.52
  22.8 0.1 copy.22
  22.9 0.1 convert_element_type.54
  23.0 0.0 copy-done.2
  23.0 0.1 and_select_fusion.2
  23.1 0.0 copy-done.10
  23.1 0.2 fusion.21
  23.3 0.2 broadcast_in_dim.42
  23.4 0.2 reshape.316
  23.7 0.0 copy-done.5
  23.7 0.0 copy-done
  23.7 0.2 convolution_negate_fusion
  24.0 0.0 copy-done.9
  24.0 0.1 copy.28
  24.1 0.0 copy-done.4
  24.1 0.1 copy.23
  24.2 0.0 copy-done.6
  24.2 0.3 fusion.32
  24.5 0.1 maximum_maximum_fusion
  24.6 0.8 copy.25
  25.4 0.1 broadcast_in_dim.48
  25.5 0.1 reshape.324
  25.6 0.8 broadcast_in_dim.50
  26.4 0.1 copy.29
  26.6 0.8 reshape.322
  27.4 0.2 concatenate.50
  27.6 0.8 fusion.9
  28.4 0.4 fusion
  28.8 0.3 reduce-precision_subtract_fusion.1
  29.2 1.4 concatenate.55
  30.6 0.0 copy-start.3
  30.6 0.1 pad_add_fusion.place_ref
  30.7 0.9 fusion.31
  31.7 0.1 select_maximum_fusion.1.vert_hbm
  31.8 0.0 copy-done.3
  31.8 0.4 fusion.1
  32.2 0.5 fusion.30
  32.7 1.3 select_maximum_fusion.wide_hbm
  34.0 43.3 %all-to-all-done.r_ref = bf16[256,8,512]{2,1,0:T(8,128)(2,1)S(1)} async-done(((bf16[256,8,512]{2,1,0:T(8,128)(2,1)}), bf16[256,8,512]{2,1,0:T(8,128)(2,1)S(1)}, u32[]{:S(2)}, u32[]{:S(2)}) %all-to-all-start) | async-done | bytes 2097184 | tf_op jit(solution)/shard_map/all_to_all | solution.py:424
  77.3 0.0 copy-start.1
  77.3 1.4 copy-done.1
  78.7 15.6 %spectral_round.1 = bf16[256,8,512]{2,1,0:T(8,128)(2,1)S(1)} custom-call(s32[11]{0:T(128)S(1)} %pad_add_fusion.place_ref, bf16[256,8,512]{2,1,0:T(8,128)(2,1)S(1)} %all-to-all-done.r_ref, f32[13,640]{1,0:T(8,128)S(1)} %pad_maximum_fusion.2.rows_ref, f32[304,320]{1,0:T(8,128)S(1)} %select_maximum_fusion.1.vert_hbm, f32[576,576]{1,0:T(8,128)S(1)} %copy-done.1, ...), custom_call_target="tpu_custom_call" | custom-call | tf_op jit(solution)/shard_map/spectral_round/pallas_call | solution.py:425
  94.3 59.2 %all_to_all.10.r_ref = bf16[256,8,512]{2,1,0:T(8,128)(2,1)S(1)} all-to-all(bf16[256,8,512]{2,1,0:T(8,128)(2,1)S(1)} %spectral_round.1), channel_id=1, replica_groups=mesh['wave'=64,'lev'=4] {'lev','wave'}, dimensions={0} | all-to-all | bytes 4194304 | tf_op jit(solution)/shard_map/all_to_all | solution.py:446
  153.5 4.3 %restore_waves.1 = bf16[36,20,2,640]{3,2,1,0:T(2,128)(2,1)} custom-call(s32[640]{0:T(1024)S(1)} %copy-done.2, bf16[256,8,512]{2,1,0:T(8,128)(2,1)S(1)} %all_to_all.10.r_ref), custom_call_target="tpu_custom_call" | custom-call | tf_op jit(solution)/shard_map/restore_waves/pallas_call | solution.py:447
  (20 shorter events, 0.2 us)
Async XLA Ops:
  0.0 23.7 %copy-start = (f32[72,72]{1,0:T(8,128)S(1)}, f32[72,72]{1,0:T(8,128)}, u32[]{:S(2)}) copy-start(f32[72,72]{1,0:T(8,128)} %param.20) | copy-start | bytes 62212
  6.7 15.8 %copy-start.8 = (f32[640]{0:T(1024)S(1)}, f32[640]{0:T(1024)}, u32[]{:S(2)}) copy-start(f32[640]{0:T(1024)} %param.16) | copy-start | bytes 7684
  6.7 15.8 %copy-start.7 = (s32[1280]{0:T(1024)S(1)}, s32[1280]{0:T(1024)}, u32[]{:S(2)}) copy-start(s32[1280]{0:T(1024)} %param.12) | copy-start | bytes 15364
  6.8 16.2 %copy-start.2 = (s32[640]{0:T(1024)S(1)}, s32[640]{0:T(1024)}, u32[]{:S(2)}) copy-start(s32[640]{0:T(1024)} %wave_ref.3) | copy-start | bytes 7684
  6.8 16.3 %copy-start.10 = (s32[64,64]{1,0:T(8,128)S(1)}, s32[64,64]{1,0:T(8,128)}, u32[]{:S(2)}) copy-start(s32[64,64]{1,0:T(8,128)} %param.14) | copy-start | bytes 49156
  6.8 16.9 %copy-start.5 = (f32[72,72]{1,0:T(8,128)S(1)}, f32[72,72]{1,0:T(8,128)}, u32[]{:S(2)}) copy-start(f32[72,72]{1,0:T(8,128)} %param.18) | copy-start | bytes 62212
  6.8 70.5 %all-to-all-start = ((bf16[256,8,512]{2,1,0:T(8,128)(2,1)}), bf16[256,8,512]{2,1,0:T(8,128)(2,1)S(1)}, u32[]{:S(2)}, u32[]{:S(2)}) async-start(bf16[256,8,512]{2,1,0:T(8,128)(2,1)} %select_waves.1), calls=%async_computation | async-start | bytes 4194304 | tf_op jit(solution)/shard_map/all_to_all | solution.py:424
  22.5 1.5 copy-start.9
  22.5 1.6 %copy-start.4 = (f32[72,72]{1,0:T(8,128)S(1)}, f32[72,72]{1,0:T(8,128)}, u32[]{:S(2)}) copy-start(f32[72,72]{1,0:T(8,128)} %param.19) | copy-start | bytes 62212
  22.5 1.7 %copy-start.6 = (f32[72,72]{1,0:T(8,128)S(1)}, f32[72,72]{1,0:T(8,128)}, u32[]{:S(2)}) copy-start(f32[72,72]{1,0:T(8,128)} %param.17) | copy-start | bytes 62212
  30.6 1.1 copy-start.3
  77.3 1.4 copy-start.1

commit v6 on v4

--- a/solution.py
+++ b/solution.py
@@ -157,13 +157,23 @@
     yield HALF, UNIT, 2 * XW + p * UNIT
 
 
+def split(values):
+    high = values.astype(BF16)
+    return high, (values - high.astype(F32)).astype(BF16)
+
+
 def solve(state_low, factor, first, second, keep, modes):
+    first_high, first_low = first
+    second_high, second_low = second
     size = modes.shape[0]
-    mixed = dot(first, jnp.concatenate([state_low, state_low], axis=0), NN)
+    mixed = dot(first_high, state_low, NN) + dot(first_low, state_low, NN)
     modal = (mixed[:size] + factor * mixed[size:]) / (1.0 + factor * modes)
-    high = modal.astype(BF16).astype(F32)
-    stacked = jnp.concatenate([high, modal - high, high], axis=0).astype(BF16)
-    new = dot(second, stacked, NN)
+    modal_high, modal_low = split(modal)
+    new = (
+        dot(second_high, modal_high, NN)
+        + dot(second_high, modal_low, NN)
+        + dot(second_low, modal_high, NN)
+    )
     return (new + keep * state_low.astype(F32)).astype(BF16)
 
 
@@ -213,10 +223,10 @@
 
     wide, narrow = (
         (
-            ref[: 2 * size, : 2 * span_in].astype(BF16),
-            ref[2 * size :, : 3 * size].astype(BF16),
-            ref[2 * size :, 3 * size : 3 * size + 1],
-            ref[2 * size : 3 * size, 3 * size + 1 : 3 * size + 2],
+            split(ref[: 2 * size, :span_in]),
+            split(ref[2 * size :, :size]),
+            ref[2 * size :, size : size + 1],
+            ref[2 * size : 3 * size, size + 1 : size + 2],
         )
         for ref, size, span_in in ((wide_ref, 2 * X, XW), (vert_ref, X, XP))
     )
@@ -300,18 +310,11 @@
 
 
 def stack_terms(first, second, keep, modes):
-    def parts(matrix):
-        high = lax.reduce_precision(matrix, 8, 7)
-        return high, matrix - high
-
-    first_high, first_low = parts(first)
-    second_high, second_low = parts(second)
     rows, size = second.shape
     column = jnp.pad(modes, (0, rows - size))[:, None]
-    top = jnp.concatenate([first_high, first_low], axis=1)
-    bottom = jnp.concatenate([second_high, second_high, second_low, keep, column], axis=1)
-    bottom = jnp.pad(bottom, ((0, 0), (0, top.shape[1] - bottom.shape[1])))
-    return jnp.concatenate([top, bottom], axis=0)
+    bottom = jnp.concatenate([second, keep, column], axis=1)
+    bottom = jnp.pad(bottom, ((0, 0), (0, first.shape[1] - bottom.shape[1])))
+    return jnp.concatenate([first, bottom], axis=0)
 
 
 def local(

time: 158 us -> 157 us (level)
  waiting for transfers between devices: 43.1 us -> 49.4 us
  local copies, waits for them, and re-layouts: 6.75 us -> 1.79 us
  other arithmetic: 3.57 us -> 0.88 us
    all_to_all x1, waiting for transfers between devices: 43.1 us -> 49.4 us  [local(): lax.all_to_all(sent, ('lev', 'wave'), split_axis=0, concat_axis=0, tiled=...]
    concatenate x2 -> x0, local copies, waits for them, and re-layouts: 1.61 us -> none  [stack_terms(): jnp.concatenate([second_high, second_high, second_low, keep, column], axi...]
  transfers between devices with their start and end apart: 1 -> 1, of which waited for: 1 -> 1; matrix products, arithmetic and copies ran while one was open for 7% -> 3% of each run, Pallas kernels for 0% -> 0%
where the time goes in v6:
time: 157 us
  blocking collectives  59.2 us (38%)
  waiting for transfers between devices  49.4 us (31%)
  Pallas kernels  26.8 us (17%)
  starting transfers between devices  15.8 us (10%)
  matrix products  2.26 us (1%)
  local copies, waits for them, and re-layouts  1.79 us (1%)
    all_to_all x1, blocking collectives, local(): lax.all_to_all(solved, ('lev', 'wave'), split_axis=0, concat_axis=0, tile...  59.2 us
    all_to_all x1, waiting for transfers between devices, local(): lax.all_to_all(sent, ('lev', 'wave'), split_axis=0, concat_axis=0, tiled=...  49.4 us
    all_to_all x1, starting transfers between devices, local(): lax.all_to_all(sent, ('lev', 'wave'), split_axis=0, concat_axis=0, tiled=...  15.8 us
    pallas_call x1, Pallas kernels, local(): pl.pallas_call(spectral_kernel, in_specs=[smem] + [vmem] * 4 + [hbm], out...  15.7 us
    pallas_call x1, Pallas kernels, local(): pl.pallas_call(select_kernel, in_specs=[vmem, hbm], out_specs=hbm, out_sh...  6.72 us
    pallas_call x1, Pallas kernels, local(): pl.pallas_call(restore_kernel, in_specs=[vmem] * 2, out_specs=hbm, out_sh...  4.34 us
  transfers between devices with their start and end apart: 1, of which 1 were waited for; matrix products, arithmetic and copies ran while one was open for 3% of the time, Pallas kernels for 0%

profile of v6, /device:TPU:1, one launch (start us, length us, event | category | flops | bytes accessed | tf_op | source)
XLA Modules:
  0.0 156.8 jit_solution(3018708959121492041)
XLA Ops:
  0.0 0.0 copy-start
  0.0 6.7 %select_waves.1 = bf16[256,8,512]{2,1,0:T(8,128)(2,1)} custom-call(s32[640]{0:T(1024)} %wave_ref.3, bf16[36,20,2,640]{3,2,1,0:T(2,128)(2,1)} %bitcast.29), custom_call_target="tpu_custom_call" | custom-call | tf_op jit(solution)/shard_map/select_waves/pallas_call | solution.py:403
  6.7 0.0 copy-start.6
  6.7 0.0 copy-start.5
  6.8 0.0 copy-start.1
  6.8 0.0 copy-start.8
  6.8 0.0 copy-start.3
  6.8 0.0 copy-start.7
  6.8 0.0 copy-start.2
  6.8 0.0 copy-start.4
  6.8 15.8 %all-to-all-start = ((bf16[256,8,512]{2,1,0:T(8,128)(2,1)}), bf16[256,8,512]{2,1,0:T(8,128)(2,1)S(1)}, u32[]{:S(2)}, u32[]{:S(2)}) async-start(bf16[256,8,512]{2,1,0:T(8,128)(2,1)} %select_waves.1), calls=%async_computation | async-start | bytes 4194304 | tf_op jit(solution)/shard_map/all_to_all | solution.py:419
  22.7 0.0 copy-done.6
  22.7 0.0 copy-done.5
  22.7 0.2 convert_element_type.52
  23.0 0.1 copy.23
  23.1 0.1 convert_element_type.54
  23.2 0.0 copy-done.1
  23.2 0.1 and_select_fusion.2
  23.3 0.0 copy-done.8
  23.3 0.2 fusion.21
  23.5 0.2 broadcast_in_dim.42
  23.6 0.2 reshape.316
  23.8 0.0 copy-done.3
  23.9 0.0 copy-done
  23.9 0.2 convolution_negate_fusion
  24.1 0.0 copy-done.7
  24.2 0.1 copy.27
  24.3 0.0 copy-done.2
  24.3 0.1 copy.24
  24.4 0.0 copy-done.4
  24.4 0.3 fusion.30
  24.7 0.1 maximum_maximum_fusion
  24.8 0.1 copy.28
  24.9 0.1 broadcast_in_dim.48
  25.0 0.1 reshape.324
  25.2 0.1 broadcast_in_dim.50
  25.3 0.1 copy.29
  25.4 0.1 reshape.322
  25.6 0.1 pad_add_fusion.place_ref
  25.7 0.1 fusion.9
  25.9 0.1 select_maximum_fusion.2
  26.0 0.4 fusion
  26.5 0.3 convolution_select_fusion.1
  26.8 0.1 select_maximum_fusion
  26.9 0.4 fusion.1
  27.3 0.5 convolution_select_fusion
  27.8 0.1 pad_maximum_fusion.wide_ref
  27.9 49.4 %all-to-all-done.r_ref = bf16[256,8,512]{2,1,0:T(8,128)(2,1)S(1)} async-done(((bf16[256,8,512]{2,1,0:T(8,128)(2,1)}), bf16[256,8,512]{2,1,0:T(8,128)(2,1)S(1)}, u32[]{:S(2)}, u32[]{:S(2)}) %all-to-all-start) | async-done | bytes 2097184 | tf_op jit(solution)/shard_map/all_to_all | solution.py:419
  77.3 15.7 %spectral_round.1 = bf16[256,8,512]{2,1,0:T(8,128)(2,1)S(1)} custom-call(s32[11]{0:T(128)S(1)} %pad_add_fusion.place_ref, bf16[256,8,512]{2,1,0:T(8,128)(2,1)S(1)} %all-to-all-done.r_ref, f32[13,640]{1,0:T(8,128)S(1)} %pad_maximum_fusion.4.rows_ref, f32[304,160]{1,0:T(8,128)S(1)} %pad_maximum_fusion.1.vert_ref, f32[576,288]{1,0:T(8,128)S(1)} %pad_maximum_fusion.wide_ref, ...), custom_call_target="tpu_custom_call" | custom-call | tf_op jit(solution)/shard_map/spectral_round/pallas_call | solution.py:420
  93.0 59.2 %all_to_all.10.r_ref = bf16[256,8,512]{2,1,0:T(8,128)(2,1)S(1)} all-to-all(bf16[256,8,512]{2,1,0:T(8,128)(2,1)S(1)} %spectral_round.1), channel_id=1, replica_groups=mesh['wave'=64,'lev'=4] {'lev','wave'}, dimensions={0} | all-to-all | bytes 4194304 | tf_op jit(solution)/shard_map/all_to_all | solution.py:438
  152.2 4.3 %restore_waves.1 = bf16[36,20,2,640]{3,2,1,0:T(2,128)(2,1)} custom-call(s32[640]{0:T(1024)S(1)} %copy-done.1, bf16[256,8,512]{2,1,0:T(8,128)(2,1)S(1)} %all_to_all.10.r_ref), custom_call_target="tpu_custom_call" | custom-call | tf_op jit(solution)/shard_map/restore_waves/pallas_call | solution.py:439
  (20 shorter events, 0.2 us)
Async XLA Ops:
  0.0 23.9 %copy-start = (f32[72,72]{1,0:T(8,128)S(1)}, f32[72,72]{1,0:T(8,128)}, u32[]{:S(2)}) copy-start(f32[72,72]{1,0:T(8,128)} %param.20) | copy-start | bytes 62212
  6.7 16.0 %copy-start.6 = (f32[640]{0:T(1024)S(1)}, f32[640]{0:T(1024)}, u32[]{:S(2)}) copy-start(f32[640]{0:T(1024)} %param.16) | copy-start | bytes 7684
  6.7 16.0 %copy-start.5 = (s32[1280]{0:T(1024)S(1)}, s32[1280]{0:T(1024)}, u32[]{:S(2)}) copy-start(s32[1280]{0:T(1024)} %param.12) | copy-start | bytes 15364
  6.8 16.4 %copy-start.1 = (s32[640]{0:T(1024)S(1)}, s32[640]{0:T(1024)}, u32[]{:S(2)}) copy-start(s32[640]{0:T(1024)} %wave_ref.3) | copy-start | bytes 7684
  6.8 16.5 %copy-start.8 = (s32[64,64]{1,0:T(8,128)S(1)}, s32[64,64]{1,0:T(8,128)}, u32[]{:S(2)}) copy-start(s32[64,64]{1,0:T(8,128)} %param.14) | copy-start | bytes 49156
  6.8 17.1 %copy-start.3 = (f32[72,72]{1,0:T(8,128)S(1)}, f32[72,72]{1,0:T(8,128)}, u32[]{:S(2)}) copy-start(f32[72,72]{1,0:T(8,128)} %param.18) | copy-start | bytes 62212
  6.8 17.4 %copy-start.7 = (f32[72]{0:T(128)S(1)}, f32[72]{0:T(128)}, u32[]{:S(2)}) copy-start(f32[72]{0:T(128)} %param.21) | copy-start | bytes 868
  6.8 17.5 %copy-start.2 = (f32[72,72]{1,0:T(8,128)S(1)}, f32[72,72]{1,0:T(8,128)}, u32[]{:S(2)}) copy-start(f32[72,72]{1,0:T(8,128)} %param.19) | copy-start | bytes 62212
  6.8 17.6 %copy-start.4 = (f32[72,72]{1,0:T(8,128)S(1)}, f32[72,72]{1,0:T(8,128)}, u32[]{:S(2)}) copy-start(f32[72,72]{1,0:T(8,128)} %param.17) | copy-start | bytes 62212
  6.8 70.5 %all-to-all-start = ((bf16[256,8,512]{2,1,0:T(8,128)(2,1)}), bf16[256,8,512]{2,1,0:T(8,128)(2,1)S(1)}, u32[]{:S(2)}, u32[]{:S(2)}) async-start(bf16[256,8,512]{2,1,0:T(8,128)(2,1)} %select_waves.1), calls=%async_computation | async-start | bytes 4194304 | tf_op jit(solution)/shard_map/all_to_all | solution.py:419
